TPU v7x, 32 devices: a whole 2x2x4 slice. The times are simulated.
32 devices in a mesh: gx: 2 (over x), gy: 8 (over z, core), gz: 2 (over y).
Axes of the slice: x: 2, y: 2, z: 4, core: 2. Of those that a mesh axis runs over, the one named last changes fastest.
Arguments:
- velocity: float32 [3, 16, 256, 256], P(None, 'gx', 'gy', 'gz'), may hold values from -6 to 6
- fibre_vel: float32 [3, 1048576], P(None, ('gx', 'gy', 'gz')), may hold values from -6 to 6
- fluid_vel: float32 [3, 1048576], P(None, ('gx', 'gy', 'gz')), may hold values from -6 to 6
- fibre_props: float32 [2, 1048576], P(None, ('gx', 'gy', 'gz')), may hold values from 0.2 to 2
- fibre_row: int32 [1048576], P(('gx', 'gy', 'gz')), may hold values from 0 to 255
- fibre_height: int32 [1048576], P(('gx', 'gy', 'gz')), may hold values from 0 to 127
- migrant_list: int32 [4, 32768], P(None, ('gx', 'gy', 'gz')), may hold values from 0 to 32767, as said below
- migrant_slot: int32 [4, 32768], P(None, ('gx', 'gy', 'gz')), may hold values from 0 to 15
- side_rows: int32 [4, 512], P(None, ('gx', 'gy', 'gz')), may hold values from 0 to 255, as said below
Outputs:
- new_velocity: float32 [3, 16, 256, 256], P(None, 'gx', 'gy', 'gz')
- kept_fibres: float32 [3, 1048576], P(None, ('gx', 'gy', 'gz'))
- arrivals: float32 [4, 3, 32768], P(None, None, ('gx', 'gy', 'gz'))
Inputs may be any that keep to these rules, and one draw needn't show every extreme that they name: `migrant_list`: the 4096 entries that one brick holds are distinct numbers of fibres of that brick. `side_rows`: row numbers x * 32 + y of the neighbour brick in the list's direction; distinct within one list of one brick. `fibre_row`: A row of the fibre's own brick; not used for a fibre that moves. `migrant_slot`: A slot of the row list of the same direction and brick.
All inputs are finite; a program needn't handle non-finite values.
Results may differ from a plain program's by a relative error of at most 0.00002.
Values sent between devices are 32-bit elements; how exact they have to be, the bound alone decides.
A program may use at most 256 MiB of HBM per device.

v0:
```python
import jax
import jax.numpy as jnp
from jax import lax
from jax.sharding import PartitionSpec as P

SWEEPS = 3


drag_step = 0.25
source_step = 1.0
coupling = 1.0


def passed_along(value, axis, steps):
    count = lax.axis_size(axis)
    pairs = [(source, (source + steps) % count) for source in range(count)]
    return lax.ppermute(value, axis, pairs)


def padded(array, sides, width):
    for axis, dim in sides:
        devices, length = (lax.axis_size(axis), array.shape[dim])
        up = [(i, (i + 1) % devices) for i in range(devices)]
        down = [(j, i) for i, j in up]
        last = lax.slice_in_dim(array, length - width, length, axis=dim)
        leading = lax.slice_in_dim(array, 0, width, axis=dim)
        before = lax.ppermute(last, axis, up)
        after = lax.ppermute(leading, axis, down)
        array = jnp.concatenate([before, array, after], axis=dim)
    return array


def fibre_terms(fibre_vel, fluid_vel, fibre_props):
    volume = fibre_props[0][None, :]
    drag_force = fibre_props[1][None, :] * (fluid_vel - fibre_vel)
    moved_vel = fibre_vel + drag_step * drag_force / volume
    partials = jnp.concatenate([drag_force, volume], axis=0)
    return (partials, moved_vel)


def adjacent_value(grid_field, axis_location, upper_value):
    leading = grid_field.ndim - 3
    result = grid_field
    for position in range(3):
        length = grid_field.shape[leading + position]
        start = 1
        if position == axis_location:
            start = 2 if upper_value else 0
        result = lax.slice_in_dim(result, start, start + length - 2, axis=leading + position)
    return result


def relaxation_pass(bordered_velocity, bordered_porosity, momentum_source):
    central_value = bordered_porosity[1:-1, 1:-1, 1:-1]
    weight_sum = jnp.zeros_like(central_value)
    flux_sum = jnp.zeros_like(momentum_source)
    for axis_location in range(3):
        for upper_value in (False, True):
            blend_weight = 0.5 * (
                central_value + adjacent_value(bordered_porosity, axis_location, upper_value)
            )
            weight_sum = weight_sum + blend_weight
            flux_sum = flux_sum + blend_weight[None] * adjacent_value(
                bordered_velocity, axis_location, upper_value
            )
    return (momentum_source + coupling * flux_sum) / (central_value + coupling * weight_sum)[None]


def wall_cells(brick_depth, margin):
    heights = (
        lax.axis_index("gz") * brick_depth
        + jnp.arange(brick_depth + 2 * margin, dtype=jnp.int32)
        - margin
    )
    return (heights < 0) | (heights >= brick_depth * lax.axis_size("gz"))


def body(
    velocity,
    fibre_vel,
    fluid_vel,
    fibre_props,
    fibre_row,
    fibre_height,
    migrant_list,
    migrant_slot,
    side_rows,
):
    width_x, width_y, width_z = (velocity.shape[1], velocity.shape[2], velocity.shape[3])
    row_count = width_x * width_y
    cell_count = row_count * width_z
    slot_count = side_rows.shape[1]
    fibre_cell = fibre_row * width_z + fibre_height
    partials, moved_vel = fibre_terms(fibre_vel, fluid_vel, fibre_props)
    staying = jnp.ones((fibre_vel.shape[1],), jnp.float32).at[migrant_list.reshape(-1)].set(0.0)
    kept_fibres = moved_vel * staying[None, :]
    deposit = (
        jnp.zeros((4, cell_count), jnp.float32).at[:, fibre_cell].add(partials * staying[None, :])
    )
    arrived = []
    for direction in range(4):
        chosen = migrant_list[direction]
        fibre_heights = fibre_height[chosen]
        step_by = 1 if direction % 2 == 1 else -1
        slot_cells = migrant_slot[direction] * width_z + fibre_heights
        row_block = (
            jnp.zeros((4, slot_count * width_z), jnp.float32)
            .at[:, slot_cells]
            .add(partials[:, chosen])
        )
        row_block = row_block.reshape(4, slot_count, width_z)
        if direction < 2:
            got_rows, got_ids, got_vel = passed_along(
                (row_block, side_rows[direction], moved_vel[:, chosen]), "gx", step_by
            )
        else:
            got_rows, got_ids, got_vel = passed_along(
                (row_block, side_rows[direction], moved_vel[:, chosen]), "gy", step_by
            )
        deposit = (
            deposit.reshape(4, row_count, width_z)
            .at[:, got_ids]
            .add(got_rows)
            .reshape(4, cell_count)
        )
        arrived.append(got_vel)
    drag_field = deposit[0:3].reshape(3, width_x, width_y, width_z)
    void_fraction = 1.0 / (1.0 + deposit[3].reshape(width_x, width_y, width_z))
    momentum_source = void_fraction[None] * velocity - source_step * drag_field
    boundary_mask = wall_cells(width_z, 1)
    bordered_field = padded(
        jnp.concatenate([velocity, void_fraction[None]], axis=0),
        (("gx", 1), ("gy", 2), ("gz", 3)),
        1,
    )
    bordered_porosity = jnp.where(boundary_mask, 1.0, bordered_field[3])
    present_velocity = relaxation_pass(
        jnp.where(boundary_mask, 0.0, bordered_field[0:3]), bordered_porosity, momentum_source
    )
    for sweep_index in range(SWEEPS - 1):
        bordered_velocity = padded(present_velocity, (("gx", 1), ("gy", 2), ("gz", 3)), 1)
        present_velocity = relaxation_pass(
            jnp.where(boundary_mask, 0.0, bordered_velocity), bordered_porosity, momentum_source
        )
    arrivals = jnp.stack(arrived, axis=0)
    return (present_velocity, kept_fibres, arrivals)


def solution(mesh):
    placed = (
        P(None, "gx", "gy", "gz"),
        P(None, ("gx", "gy", "gz")),
        P(None, ("gx", "gy", "gz")),
        P(None, ("gx", "gy", "gz")),
        P(("gx", "gy", "gz")),
        P(("gx", "gy", "gz")),
        P(None, ("gx", "gy", "gz")),
        P(None, ("gx", "gy", "gz")),
        P(None, ("gx", "gy", "gz")),
    )
    return jax.shard_map(
        body,
        mesh=mesh,
        in_specs=placed,
        out_specs=(
            P(None, "gx", "gy", "gz"),
            P(None, ("gx", "gy", "gz")),
            P(None, None, ("gx", "gy", "gz")),
        ),
        check_vma=False,
    )
```

profile of v0, /device:TPU:0, one launch (start us, length us, event | category | flops | bytes accessed | tf_op | source)
XLA Modules:
  0.0 540.4 jit_solution(13405690292087467533)
XLA Ops:
  1.9 2.5 collective-permute-start.2
  4.5 3.2 collective-permute-start.4
  9.4 5.9 %gather_fusion.2 = s32[1024]{0:T(1024)S(1)} fusion(s32[32768]{0:T(1024)} %param.14, s32[1024]{0:T(1024)S(1)} %broadcast_clamp_fusion.1), kind=kCustom, calls=%fused_computation.4 | custom fusion | bytes 12288 | tf_op jit(solution)/shard_map/gather | solution.py:103
  15.4 6.2 %gather_fusion = s32[1024]{0:T(1024)S(1)} fusion(s32[32768]{0:T(1024)S(1)} %copy-done, s32[1024]{0:T(1024)S(1)} %broadcast_clamp_fusion.3), kind=kCustom, calls=%fused_computation | custom fusion | bytes 12288 | tf_op jit(solution)/shard_map/gather | solution.py:103
  21.6 6.2 %gather_fusion.1 = s32[1024]{0:T(1024)S(1)} fusion(s32[32768]{0:T(1024)S(1)} %copy-done, s32[1024]{0:T(1024)S(1)} %broadcast_clamp_fusion.2), kind=kCustom, calls=%fused_computation.2 | custom fusion | bytes 12288 | tf_op jit(solution)/shard_map/gather | solution.py:103
  27.7 6.2 %gather_fusion.3 = s32[1024]{0:T(1024)S(1)} fusion(s32[32768]{0:T(1024)S(1)} %copy-done, s32[1024]{0:T(1024)S(1)} %broadcast_clamp_fusion), kind=kCustom, calls=%fused_computation.6 | custom fusion | bytes 12288 | tf_op jit(solution)/shard_map/gather | solution.py:103
  34.1 8.1 %copy.144 = f32[1,32768]{0,1:T(8,128)} copy(f32[1,32768]{1,0:T(1,128)S(1)} %get-tuple-element.49) | data formatting | bytes 262144
  42.2 8.5 %copy.106 = f32[3,32768]{0,1:T(8,128)} copy(f32[3,32768]{1,0:T(4,128)S(1)} %copy-done.28) | data formatting | bytes 786432 | tf_op args[1]
  50.7 8.4 %copy.105 = f32[3,32768]{0,1:T(8,128)} copy(f32[3,32768]{1,0:T(4,128)S(1)} %copy-done.29) | data formatting | bytes 786432 | tf_op args[2]
  59.2 15.6 %scatter_custom_fusion = f32[32768]{0:T(1024)S(1)} fusion(s32[4096]{0:T(1024)S(1)} %bitcast.101, f32[4096]{0:T(1024)S(1)} %broadcast.231, f32[]{:T(128)} %constant.11.clone.1), kind=kCustom, calls=%fused_computation.115 | custom fusion | bytes 131076 | tf_op jit(solution)/shard_map/scatter | solution.py:95
  74.7 28.4 %broadcast_multiply_fusion = (f32[3,32768]{0,1:T(8,128)}, f32[3,32768]{0,1:T(8,128)}, f32[3,32768]{0,1:T(8,128)}) fusion(f32[32768]{0:T(1024)S(1)} %scatter_custom_fusion, f32[3,32768]{0,1:T(8,128)} %copy.106, f32[32768]{0:T(1024)S(1)} %bitcast.89, f32[3,32768]{0,1:T(8,128)} %copy.105, f32[32768]{0:T(1024)S(1)} %bitcast.90), kind=kLoop, calls=%fused_computation.28 | loop fusion | flops 589824 | bytes 2359296 | tf_op jit(solution)/shard_map/mul | solution.py:96
  103.2 17.3 %pad_maximum_fusion = f32[4,32768]{0,1:T(8,128)} fusion(f32[1,32768]{0,1:T(8,128)} %copy.144, f32[3,32768]{0,1:T(8,128)} %get-tuple-element.20), kind=kLoop, calls=%fused_computation.22 | loop fusion | flops 131072 | bytes 1048576 | tf_op jit(solution)/shard_map/concatenate | solution.py:37
  120.5 12.1 %scatter_custom_fusion.6 = f32[4,2048]{0,1:T(8,128)S(1)} fusion(s32[1024]{0:T(1024)S(1)} %bitcast.113, f32[]{:T(128)} %constant.12.clone.1, f32[4,32768]{0,1:T(8,128)} %pad_maximum_fusion, s32[1024]{0:T(1024)S(1)} %broadcast_clamp_fusion.1), kind=kCustom, calls=%fused_computation.42 | custom fusion | flops 4096 | bytes 33280 | tf_op jit(solution)/shard_map/scatter-add | solution.py:109
  132.9 1.3 collective-permute-start.5
  134.3 198.2 %scatter_custom_fusion.1 = f32[4,32768]{0,1:T(8,128)} fusion(s32[32768]{0:T(1024)S(1)} %compare_select_fusion, f32[32768]{0:T(1024)S(1)} %scatter_custom_fusion, f32[]{:T(128)} %constant.12.clone.1, f32[1,32768]{0,1:T(8,128)} %copy.144, f32[3,32768]{0,1:T(8,128)} %get-tuple-element.20), kind=kCustom, calls=%fused_computation.23 | custom fusion | flops 393216 | bytes 1179652 | tf_op jit(solution)/shard_map/scatter-add | solution.py:98
  332.5 9.4 %copy.109 = f32[4,256,128]{2,0,1:T(4,128)S(1)} copy(f32[4,256,128]{0,2,1:T(8,128)} %bitcast.80) | data formatting | bytes 1048576 | tf_op jit(solution)/shard_map/reshape | solution.py:121
  341.9 12.1 %scatter_custom_fusion.4 = f32[4,2048]{0,1:T(8,128)S(1)} fusion(s32[1024]{0:T(1024)S(1)} %bitcast.112, f32[]{:T(128)} %constant.12.clone.1, f32[4,32768]{0,1:T(8,128)} %pad_maximum_fusion, s32[1024]{0:T(1024)S(1)} %broadcast_clamp_fusion.2), kind=kCustom, calls=%fused_computation.44 | custom fusion | flops 4096 | bytes 33280 | tf_op jit(solution)/shard_map/scatter-add | solution.py:109
  354.3 12.6 %scatter_custom_fusion.2 = f32[4,2048]{0,1:T(8,128)S(1)} fusion(s32[1024]{0:T(1024)S(1)} %bitcast.111, f32[]{:T(128)} %constant.12.clone.1, f32[4,32768]{0,1:T(8,128)} %pad_maximum_fusion, s32[1024]{0:T(1024)S(1)} %broadcast_clamp_fusion.3), kind=kCustom, calls=%fused_computation.46 | custom fusion | flops 4096 | bytes 33280 | tf_op jit(solution)/shard_map/scatter-add | solution.py:109
  366.9 12.1 %scatter_custom_fusion.8 = f32[4,2048]{0,1:T(8,128)S(1)} fusion(s32[1024]{0:T(1024)S(1)} %bitcast.110, f32[]{:T(128)} %constant.12.clone.1, f32[4,32768]{0,1:T(8,128)} %pad_maximum_fusion, s32[1024]{0:T(1024)S(1)} %broadcast_clamp_fusion), kind=kCustom, calls=%fused_computation.40 | custom fusion | flops 4096 | bytes 33280 | tf_op jit(solution)/shard_map/scatter-add | solution.py:109
  379.6 1.5 collective-permute-start.3
  381.8 3.3 collective-permute-done.1
  385.0 1.1 scatter_fusion
  386.2 1.1 scatter_fusion.1
  387.3 1.1 scatter_fusion.2
  388.4 1.1 scatter_fusion.3
  390.4 1.4 collective-permute-start.9
  391.8 2.2 collective-permute-done.8
  394.9 3.7 collective-permute-start.11
  398.6 2.9 copy.117
  401.5 3.0 copy.116
  404.5 2.9 copy.118
  407.4 6.9 %pad_maximum_fusion.1 = f32[4,10,34,128]{2,1,3,0:T(8,128)S(1)} fusion(f32[4,10,1,128]{2,1,3,0:T(8,128)} %copy.118, f32[4,10,32,128]{2,1,3,0:T(8,128)} %copy.117, f32[4,10,1,128]{2,1,3,0:T(8,128)} %copy.116), kind=kLoop, calls=%fused_computation.31 | loop fusion | flops 348160 | bytes 1392640 | tf_op jit(solution)/shard_map/concatenate | solution.py:29
  414.3 2.0 copy-done.1
  416.3 1.5 collective-permute-start.12
  418.3 2.7 copy.120
  424.5 1.3 collective-permute-start.14
  426.5 2.1 collective-permute-done.14
  428.6 1.3 collective-permute-done.15
  430.0 3.7 collective-permute-start.17
  433.8 2.3 copy.125
  436.1 2.3 copy.124
  438.4 2.2 copy.126
  440.6 5.4 %pad_maximum_fusion.2 = f32[3,10,34,128]{2,1,3,0:T(8,128)S(1)} fusion(f32[3,10,1,128]{2,1,3,0:T(8,128)} %copy.126, f32[3,10,32,128]{2,1,3,0:T(8,128)} %copy.125, f32[3,10,1,128]{2,1,3,0:T(8,128)} %copy.124), kind=kLoop, calls=%fused_computation.32 | loop fusion | flops 261120 | bytes 1044480 | tf_op jit(solution)/shard_map/concatenate | solution.py:29
  447.5 1.2 collective-permute-start.18
  448.7 1.9 copy.128
  450.8 1.2 copy.129
  453.1 1.6 maximum_select_fusion
  456.2 1.3 collective-permute-start.21
  457.5 8.6 %gather_fusion.4 = f32[1024,3]{1,0:T(8,128)S(1)} fusion(f32[3,32768]{0,1:T(8,128)} %get-tuple-element.19, s32[1024]{0:T(1024)S(1)} %broadcast_clamp_fusion.3), kind=kCustom, calls=%fused_computation.8 | custom fusion | bytes 28672 | tf_op jit(solution)/shard_map/gather | solution.py:114
  467.1 3.5 collective-permute-start.23
  470.6 9.8 %gather_fusion.7 = f32[1024,3]{1,0:T(8,128)} fusion(f32[3,32768]{0,1:T(8,128)} %get-tuple-element.19, s32[1024]{0:T(1024)S(1)} %broadcast_clamp_fusion), kind=kCustom, calls=%fused_computation.11 | custom fusion | bytes 28672 | tf_op jit(solution)/shard_map/gather | solution.py:118
  480.3 9.8 %gather_fusion.5 = f32[1024,3]{1,0:T(8,128)} fusion(f32[3,32768]{0,1:T(8,128)} %get-tuple-element.19, s32[1024]{0:T(1024)S(1)} %broadcast_clamp_fusion.2), kind=kCustom, calls=%fused_computation.9 | custom fusion | bytes 28672 | tf_op jit(solution)/shard_map/gather | solution.py:114
  490.1 1.3 collective-permute-start.27
  491.4 9.8 %gather_fusion.6 = f32[1024,3]{1,0:T(8,128)} fusion(f32[3,32768]{0,1:T(8,128)} %get-tuple-element.19, s32[1024]{0:T(1024)S(1)} %broadcast_clamp_fusion.1), kind=kCustom, calls=%fused_computation.10 | custom fusion | bytes 28672 | tf_op jit(solution)/shard_map/gather | solution.py:118
  501.2 3.5 collective-permute-start.28
  504.6 9.8 %copy.143 = f32[3,32768]{1,0:T(4,128)} copy(f32[3,32768]{0,1:T(8,128)} %get-tuple-element.18) | data formatting | bytes 786432
  517.0 2.3 copy.133
  519.3 2.3 copy.132
  521.6 2.2 copy.134
  523.9 5.5 %pad_maximum_fusion.3 = f32[3,10,34,128]{2,1,3,0:T(8,128)S(1)} fusion(f32[3,10,1,128]{2,1,3,0:T(8,128)} %copy.134, f32[3,10,32,128]{2,1,3,0:T(8,128)} %copy.133, f32[3,10,1,128]{2,1,3,0:T(8,128)} %copy.132), kind=kLoop, calls=%fused_computation.33 | loop fusion | flops 261120 | bytes 1044480 | tf_op jit(solution)/shard_map/concatenate | solution.py:29
  530.8 1.2 collective-permute-start.25
  532.7 1.9 copy.136
  537.1 1.6 maximum_select_fusion.1
  538.8 1.4 fusion.21
  (171 shorter events, 23.9 us)
Async XLA Ops:
  0.6 14.7 %copy-start = (s32[32768]{0:T(1024)S(1)}, s32[32768]{0:T(1024)}, u32[]{:S(2)}) copy-start(s32[32768]{0:T(1024)} %param.14) | copy-start | bytes 393220
  1.5 378.2 %collective-permute-start.6 = (s32[16]{0:T(128)S(1)}, s32[16]{0:T(128)S(1)}, u32[]{:S(2)}, u32[]{:S(2)}) collective-permute-start(s32[16]{0:T(128)S(1)} %get-tuple-element.58), channel_id=1, source_target_pairs={{0,2},{2,4},{4,6},{6,8},{8,10},{10,12},{12,14},{14,0},{1,3},{3,5},... | collective-permute-start | bytes 200 | tf_op jit(solution)/shard_map/ppermute | solution.py:17
  1.9 379.2 %collective-permute-start.2 = (s32[16]{0:T(128)S(1)}, s32[16]{0:T(128)S(1)}, u32[]{:S(2)}, u32[]{:S(2)}) collective-permute-start(s32[16]{0:T(128)S(1)} %get-tuple-element.59), channel_id=1, source_target_pairs={{0,16},{16,0},{1,17},{17,1},{2,18},{18,2},{3,19},{19,3},{4,20},{20... | collective-permute-start | bytes 200 | tf_op jit(solution)/shard_map/ppermute | solution.py:17
  4.5 377.3 %collective-permute-start = (s32[16]{0:T(128)S(1)}, s32[16]{0:T(128)S(1)}, u32[]{:S(2)}, u32[]{:S(2)}) collective-permute-start(s32[16]{0:T(128)S(1)} %get-tuple-element.60), channel_id=1, source_target_pairs={{0,16},{16,0},{1,17},{17,1},{2,18},{18,2},{3,19},{19,3},{4,20},{20... | collective-permute-start | bytes 200 | tf_op jit(solution)/shard_map/ppermute | solution.py:17
  4.5 377.2 %collective-permute-start.4 = (s32[16]{0:T(128)S(1)}, s32[16]{0:T(128)S(1)}, u32[]{:S(2)}, u32[]{:S(2)}) collective-permute-start(s32[16]{0:T(128)S(1)} %get-tuple-element.61), channel_id=1, source_target_pairs={{0,14},{2,0},{4,2},{6,4},{8,6},{10,8},{12,10},{14,12},{1,15},{3,1}... | collective-permute-start | bytes 200 | tf_op jit(solution)/shard_map/ppermute | solution.py:17
  21.5 12.3 %copy-start.30 = (f32[2,32768]{1,0:T(2,128)S(1)}, f32[2,32768]{1,0:T(2,128)}, u32[]{:S(2)}) copy-start(f32[2,32768]{1,0:T(2,128)} %param.12) | copy-start | bytes 786436
  34.1 8.1 %copy-start.28 = (f32[3,32768]{1,0:T(4,128)S(1)}, f32[3,32768]{1,0:T(4,128)}, u32[]{:S(2)}) copy-start(f32[3,32768]{1,0:T(4,128)} %param.10) | copy-start | bytes 1179652
  42.2 8.5 %copy-start.29 = (f32[3,32768]{1,0:T(4,128)S(1)}, f32[3,32768]{1,0:T(4,128)}, u32[]{:S(2)}) copy-start(f32[3,32768]{1,0:T(4,128)} %param.11) | copy-start | bytes 1179652
  103.1 17.3 %copy-start.35 = (s32[4,1024]{1,0:T(4,128)S(1)}, s32[4,1024]{1,0:T(4,128)}, u32[]{:S(2)}) copy-start(s32[4,1024]{1,0:T(4,128)} %param.16) | copy-start | bytes 49156
  103.2 31.1 %copy-start.31 = (s32[32768]{0:T(1024)S(1)}, s32[32768]{0:T(1024)}, u32[]{:S(2)}) copy-start(s32[32768]{0:T(1024)} %param.13) | copy-start | bytes 393220
  132.9 254.3 %collective-permute-start.5 = (f32[4,16,128]{2,0,1:T(4,128)S(1)}, f32[4,16,128]{2,0,1:T(4,128)S(1)}, u32[]{:S(2)}, u32[]{:S(2)}) collective-permute-start(f32[4,16,128]{2,0,1:T(4,128)S(1)} %copy.111), channel_id=1, source_target_pairs={{0,14},{2,0},{4,2},{6,4},{8,6},{10,8},{12,10},{14,12},{1,15},{3,1}... | collective-permute-start | bytes 98312 | tf_op jit(solution)/shard_map/ppermute | solution.py:17
  341.9 47.8 %copy-start.2 = (f32[3,8,32,128]{3,2,1,0:T(8,128)S(1)}, f32[3,8,32,128]{3,2,1,0:T(8,128)}, u32[]{:S(2)}) copy-start(f32[3,8,32,128]{3,2,1,0:T(8,128)} %param.9) | copy-start | bytes 1179652
  379.6 6.5 %collective-permute-start.3 = (f32[4,16,128]{2,0,1:T(4,128)S(1)}, f32[4,16,128]{2,0,1:T(4,128)S(1)}, u32[]{:S(2)}, u32[]{:S(2)}) collective-permute-start(f32[4,16,128]{2,0,1:T(4,128)S(1)} %copy.110), channel_id=1, source_target_pairs={{0,16},{16,0},{1,17},{17,1},{2,18},{18,2},{3,19},{19,3},{4,20},{20... | collective-permute-start | bytes 98312 | tf_op jit(solution)/shard_map/ppermute | solution.py:17
  381.1 3.9 collective-permute-start.1
  381.7 6.6 %collective-permute-start.7 = (f32[4,16,128]{2,0,1:T(4,128)S(1)}, f32[4,16,128]{2,0,1:T(4,128)S(1)}, u32[]{:S(2)}, u32[]{:S(2)}) collective-permute-start(f32[4,16,128]{2,0,1:T(4,128)S(1)} %copy.112), channel_id=1, source_target_pairs={{0,2},{2,4},{4,6},{6,8},{8,10},{10,12},{12,14},{14,0},{1,3},{3,5},... | collective-permute-start | bytes 98312 | tf_op jit(solution)/shard_map/ppermute | solution.py:17
  389.5 15.0 %copy-start.3 = (f32[4,256,128]{2,0,1:T(4,128)}, f32[4,256,128]{2,0,1:T(4,128)S(1)}, u32[]{:S(2)}) copy-start(f32[4,256,128]{2,0,1:T(4,128)S(1)} %scatter_fusion.3) | copy-start | bytes 1572868
  389.7 14.8 %copy-start.26 = (f32[1,256,128]{2,0,1:T(1,128)}, f32[1,256,128]{2,0,1:T(1,128)S(1)}, u32[]{:S(2)}) copy-start(f32[1,256,128]{2,0,1:T(1,128)S(1)} %fusion.46) | copy-start | bytes 393220
  389.7 4.3 collective-permute-start.8
  390.4 4.4 collective-permute-start.9
  394.8 6.7 %collective-permute-start.10 = (f32[4,10,1,128]{3,1,2,0:T(8,128)S(1)}, f32[4,10,1,128]{3,1,2,0:T(8,128)S(1)}, u32[]{:S(2)}, u32[]{:S(2)}) collective-permute-start(f32[4,10,1,128]{3,1,2,0:T(8,128)S(1)} %copy.145), channel_id=1, source_target_pairs={{0,2},{2,4},{4,6},{6,8},{8,10},{10,12},{12,14},{14,0},{1,3},{3,5},... | collective-permute-start | bytes 61448 | tf_op jit(solution)/shard_map/ppermute | solution.py:27
  394.9 9.6 %collective-permute-start.11 = (f32[4,10,1,128]{3,1,2,0:T(8,128)S(1)}, f32[4,10,1,128]{3,1,2,0:T(8,128)S(1)}, u32[]{:S(2)}, u32[]{:S(2)}) collective-permute-start(f32[4,10,1,128]{3,1,2,0:T(8,128)S(1)} %copy.146), channel_id=1, source_target_pairs={{2,0},{4,2},{6,4},{8,6},{10,8},{12,10},{14,12},{0,14},{3,1},{5,3},... | collective-permute-start | bytes 61448 | tf_op jit(solution)/shard_map/ppermute | solution.py:28
  414.3 2.0 copy-start.1
  416.3 5.9 %collective-permute-start.12 = (f32[4,10,34,1]{2,1,3,0:T(8,128)S(1)}, f32[4,10,34,1]{2,1,3,0:T(8,128)S(1)}, u32[]{:S(2)}, u32[]{:S(2)}) collective-permute-start(f32[4,10,34,1]{2,1,3,0:T(8,128)S(1)} %get-tuple-element.30), channel_id=1, source_target_pairs={{0,1},{1,0},{2,3},{3,2},{4,5},{5,4},{6,7},{7,6},{8,9},{9,8},{10,11... | collective-permute-start | bytes 16328 | tf_op jit(solution)/shard_map/ppermute | solution.py:27
  417.8 3.9 collective-permute-start.13
  418.3 4.5 copy-start.36
  422.5 1.2 copy-start.4
  422.6 1.2 copy-start.27
  423.7 2.1 copy-start.23
  423.7 12.4 %copy-start.5 = (f32[8,32,128]{2,1,0:T(8,128)}, f32[8,32,128]{2,1,0:T(8,128)S(1)}, u32[]{:S(2)}) copy-start(f32[8,32,128]{2,1,0:T(8,128)S(1)} %get-tuple-element.23) | copy-start | bytes 393220
  423.7 12.4 %copy-start.8 = (f32[8,32,128]{2,1,0:T(8,128)}, f32[8,32,128]{2,1,0:T(8,128)S(1)}, u32[]{:S(2)}) copy-start(f32[8,32,128]{2,1,0:T(8,128)S(1)} %get-tuple-element.24) | copy-start | bytes 393220
  424.5 4.1 collective-permute-start.14
  425.8 4.1 collective-permute-start.15
  430.0 6.1 %collective-permute-start.16 = (f32[3,10,1,128]{3,1,2,0:T(8,128)S(1)}, f32[3,10,1,128]{3,1,2,0:T(8,128)S(1)}, u32[]{:S(2)}, u32[]{:S(2)}) collective-permute-start(f32[3,10,1,128]{3,1,2,0:T(8,128)S(1)} %copy.147), channel_id=1, source_target_pairs={{0,2},{2,4},{4,6},{6,8},{8,10},{10,12},{12,14},{14,0},{1,3},{3,5},... | collective-permute-start | bytes 46088 | tf_op jit(solution)/shard_map/ppermute | solution.py:27
  430.0 8.3 %collective-permute-start.17 = (f32[3,10,1,128]{3,1,2,0:T(8,128)S(1)}, f32[3,10,1,128]{3,1,2,0:T(8,128)S(1)}, u32[]{:S(2)}, u32[]{:S(2)}) collective-permute-start(f32[3,10,1,128]{3,1,2,0:T(8,128)S(1)} %copy.148), channel_id=1, source_target_pairs={{2,0},{4,2},{6,4},{8,6},{10,8},{12,10},{14,12},{0,14},{3,1},{5,3},... | collective-permute-start | bytes 46088 | tf_op jit(solution)/shard_map/ppermute | solution.py:28
  446.6 4.1 collective-permute-start.19
  447.5 4.5 collective-permute-start.18
  450.6 4.1 copy-start.6
  450.6 4.1 copy-start.9
  450.6 4.1 copy-start.12
  450.6 4.2 copy-start.15
  450.6 4.2 copy-start.18
  450.6 4.2 copy-start.21
  450.6 4.2 copy-start.24
  455.4 11.4 %collective-permute-start.20 = (f32[3,1,32,128]{3,2,1,0:T(8,128)S(1)}, f32[3,1,32,128]{3,2,1,0:T(8,128)S(1)}, u32[]{:S(2)}, u32[]{:S(2)}) collective-permute-start(f32[3,1,32,128]{3,2,1,0:T(8,128)S(1)} %get-tuple-element.44), channel_id=1, source_target_pairs={{0,16},{16,0},{1,17},{17,1},{2,18},{18,2},{3,19},{19,3},{4,20},{20... | collective-permute-start | bytes 147464 | tf_op jit(solution)/shard_map/ppermute | solution.py:27
  456.2 10.7 %collective-permute-start.21 = (f32[3,1,32,128]{3,2,1,0:T(8,128)S(1)}, f32[3,1,32,128]{3,2,1,0:T(8,128)S(1)}, u32[]{:S(2)}, u32[]{:S(2)}) collective-permute-start(f32[3,1,32,128]{3,2,1,0:T(8,128)S(1)} %get-tuple-element.45), channel_id=1, source_target_pairs={{16,0},{0,16},{17,1},{1,17},{18,2},{2,18},{19,3},{3,19},{20,4},{4,... | collective-permute-start | bytes 147464 | tf_op jit(solution)/shard_map/ppermute | solution.py:28
  466.1 35.0 %collective-permute-start.26 = (f32[3,1024]{0,1:T(8,128)S(1)}, f32[3,1024]{0,1:T(8,128)S(1)}, u32[]{:S(2)}, u32[]{:S(2)}) collective-permute-start(f32[3,1024]{0,1:T(8,128)S(1)} %bitcast.114), channel_id=1, source_target_pairs={{0,16},{16,0},{1,17},{17,1},{2,18},{18,2},{3,19},{19,3},{4,20},{20... | collective-permute-start | bytes 36872 | tf_op jit(solution)/shard_map/ppermute | solution.py:17
  467.0 52.4 %collective-permute-start.22 = (f32[3,10,1,128]{3,1,2,0:T(8,128)S(1)}, f32[3,10,1,128]{3,1,2,0:T(8,128)S(1)}, u32[]{:S(2)}, u32[]{:S(2)}) collective-permute-start(f32[3,10,1,128]{3,1,2,0:T(8,128)S(1)} %copy.149), channel_id=1, source_target_pairs={{0,2},{2,4},{4,6},{6,8},{8,10},{10,12},{12,14},{14,0},{1,3},{3,5},... | collective-permute-start | bytes 46088 | tf_op jit(solution)/shard_map/ppermute | solution.py:27
  467.1 54.6 %collective-permute-start.23 = (f32[3,10,1,128]{3,1,2,0:T(8,128)S(1)}, f32[3,10,1,128]{3,1,2,0:T(8,128)S(1)}, u32[]{:S(2)}, u32[]{:S(2)}) collective-permute-start(f32[3,10,1,128]{3,1,2,0:T(8,128)S(1)} %copy.150), channel_id=1, source_target_pairs={{2,0},{4,2},{6,4},{8,6},{10,8},{12,10},{14,12},{0,14},{3,1},{5,3},... | collective-permute-start | bytes 46088 | tf_op jit(solution)/shard_map/ppermute | solution.py:28
  480.3 34.3 %collective-permute-start.29 = (f32[3,1024]{0,1:T(8,128)}, f32[3,1024]{0,1:T(8,128)S(1)}, u32[]{:S(2)}, u32[]{:S(2)}) collective-permute-start(f32[3,1024]{0,1:T(8,128)} %bitcast.46), channel_id=1, source_target_pairs={{0,2},{2,4},{4,6},{6,8},{8,10},{10,12},{12,14},{14,0},{1,3},{3,5},... | collective-permute-start | bytes 36872 | tf_op jit(solution)/shard_map/ppermute | solution.py:17
  490.1 25.4 %collective-permute-start.27 = (f32[3,1024]{0,1:T(8,128)}, f32[3,1024]{0,1:T(8,128)S(1)}, u32[]{:S(2)}, u32[]{:S(2)}) collective-permute-start(f32[3,1024]{0,1:T(8,128)} %bitcast.115), channel_id=1, source_target_pairs={{0,16},{16,0},{1,17},{17,1},{2,18},{18,2},{3,19},{19,3},{4,20},{20... | collective-permute-start | bytes 36872 | tf_op jit(solution)/shard_map/ppermute | solution.py:17
  501.2 15.1 %collective-permute-start.28 = (f32[3,1024]{0,1:T(8,128)}, f32[3,1024]{0,1:T(8,128)S(1)}, u32[]{:S(2)}, u32[]{:S(2)}) collective-permute-start(f32[3,1024]{0,1:T(8,128)} %bitcast.116), channel_id=1, source_target_pairs={{0,14},{2,0},{4,2},{6,4},{8,6},{10,8},{12,10},{14,12},{1,15},{3,1}... | collective-permute-start | bytes 36872 | tf_op jit(solution)/shard_map/ppermute | solution.py:17
  523.9 8.1 %copy-start.32 = (f32[1,3,1024]{2,0,1:T(1,128)S(1)}, f32[1,3,1024]{2,0,1:T(1,128)}, u32[]{:S(2)}) copy-start(f32[1,3,1024]{2,0,1:T(1,128)} %copy.142) | copy-start | bytes 36868
  523.9 8.1 %copy-start.33 = (f32[1,3,1024]{2,0,1:T(1,128)S(1)}, f32[1,3,1024]{2,0,1:T(1,128)}, u32[]{:S(2)}) copy-start(f32[1,3,1024]{2,0,1:T(1,128)} %copy.140) | copy-start | bytes 36868
  523.9 8.1 %copy-start.34 = (f32[1,3,1024]{2,0,1:T(1,128)S(1)}, f32[1,3,1024]{2,0,1:T(1,128)}, u32[]{:S(2)}) copy-start(f32[1,3,1024]{2,0,1:T(1,128)} %copy.141) | copy-start | bytes 36868
  529.3 7.8 %copy-start.37 = (pred[130]{0:T(512)(128)(4,1)S(1)}, pred[130]{0:T(512)(128)(4,1)}, u32[]{:S(2)}) copy-start(pred[130]{0:T(512)(128)(4,1)} %copy-done.36) | copy-start | bytes 394
  530.0 6.1 %collective-permute-start.24 = (f32[3,10,34,1]{2,1,3,0:T(8,128)}, f32[3,10,34,1]{2,1,3,0:T(8,128)}, u32[]{:S(2)}, u32[]{:S(2)}) collective-permute-start(f32[3,10,34,1]{2,1,3,0:T(8,128)} %get-tuple-element.32), channel_id=1, source_target_pairs={{0,1},{1,0},{2,3},{3,2},{4,5},{5,4},{6,7},{7,6},{8,9},{9,8},{10,11... | collective-permute-start | bytes 12248 | tf_op jit(solution)/shard_map/ppermute | solution.py:27
  530.8 4.1 collective-permute-start.25
  534.6 4.1 copy-start.7
  534.6 4.2 copy-start.10
  534.6 4.2 copy-start.13
  534.6 4.2 copy-start.16
  534.6 4.2 copy-start.19
  534.6 4.2 copy-start.22
  534.6 4.2 copy-start.25
  (4 other events, 2.9 us)
where the time goes:
time: 549 us; the launch traced here: 540 us
  other arithmetic  324 us (59%)
  local copies, waits for them, and re-layouts  166 us (30%)
  starting transfers between devices  38.6 us (7%)
  waiting for transfers between devices  10.8 us (2%)
    scatter-add x1, other arithmetic, body(): jnp.zeros((4, cell_count), jnp.float32).at[:, fibre_cell]  198 us
    scatter-add x4, other arithmetic, body(): row_block = jnp.zeros((4, slot_count * width_z), jnp.float32).at[:, slot_...  48.8 us
    unnamed x87, local copies, waits for them, and re-layouts  37.9 us
    gather x4, local copies, waits for them, and re-layouts, body(): moved_vel[:, chosen]  37.8 us
    mul x1, other arithmetic, body(): kept_fibres = moved_vel * staying[None, :]  28.4 us
    gather x4, local copies, waits for them, and re-layouts, body(): fibre_heights = fibre_height[chosen]  24.4 us
    concatenate x6, other arithmetic, padded(): array = jnp.concatenate([before, array, after], axis=dim)  17.9 us
    concatenate x1, other arithmetic, fibre_terms(): partials = jnp.concatenate([drag_force, volume], axis=0)  17.3 us
  transfers between devices with their start and end apart: 30, of which 8 were waited for; matrix products, arithmetic and copies ran while one was open for 83% of the time, Pallas kernels for 0%

commit v1 on v0

--- a/solution.py
+++ b/solution.py
@@ -1,14 +1,232 @@
 import jax
 import jax.numpy as jnp
 from jax import lax
+from jax.experimental import pallas as pl
+from jax.experimental.pallas import tpu as pltpu
 from jax.sharding import PartitionSpec as P
 
 SWEEPS = 3
-
-
 drag_step = 0.25
 source_step = 1.0
 coupling = 1.0
+F32, BF16 = jnp.float32, jnp.bfloat16
+LANES = 128
+GROUP = 16
+NT = (((1,), (1,)), ((), ()))
+
+
+def parts_of(value):
+    high = value.astype(BF16)
+    low = (value - high.astype(F32)).astype(BF16)
+    return high, low
+
+
+def spread16(row):
+    return jnp.broadcast_to(row, (16, row.shape[1])).astype(BF16)
+
+
+def one_hot(row16, count, iota16):
+    blocks = count // 16
+    n = row16.shape[1]
+    out = []
+    for block in range(blocks):
+        hit = iota16 == row16 - float(block * 16)
+        out.append(jnp.where(hit, jnp.ones((), BF16), jnp.zeros((), BF16)))
+    return jnp.concatenate(out, axis=0)
+
+
+def local_kernel(
+    vel, flu, prop, row, height, mlist, mslot, side,
+    kept, dep, rows, mov,
+    st_vel, st_flu, st_prop, tabs, moved_t, gt_hi, gt_lo, gath, b0, a0, b1, a1, acc,
+):
+    groups = row.shape[0]
+    row_count = dep.shape[1]
+    migs = mlist.shape[1]
+    slots = side.shape[1]
+
+    def stage(step, carry):
+        for k in range(8):
+            g = step * 8 + k
+            at = pl.multiple_of(g * LANES, LANES)
+            to = pl.multiple_of(g * 8, 8)
+            st_vel[pl.ds(to, 3), :] = vel[:, pl.ds(at, LANES)]
+            st_flu[pl.ds(to, 3), :] = flu[:, pl.ds(at, LANES)]
+            st_prop[pl.ds(to, 2), :] = prop[:, pl.ds(at, LANES)]
+        return carry
+
+    lax.fori_loop(0, groups // 8, stage, 0)
+
+    lists = mlist[...]
+    list_hi = (lists // LANES).astype(F32)
+    list_lo = (lists % LANES).astype(F32)
+    iota16 = lax.broadcasted_iota(jnp.int32, (16, migs), 0).astype(F32).astype(BF16)
+    named = jnp.zeros((groups, LANES), F32)
+    for d in range(4):
+        named = named + lax.dot_general(
+            one_hot(spread16(list_hi[d:d + 1]), groups, iota16),
+            one_hot(spread16(list_lo[d:d + 1]), LANES, iota16),
+            NT, preferred_element_type=F32,
+        )
+    leaves = named > 0.5
+
+    volume = st_prop[pl.ds(0, groups, stride=8), :]
+    beta = st_prop[pl.ds(1, groups, stride=8), :]
+    for c in range(3):
+        v = st_vel[pl.ds(c, groups, stride=8), :]
+        f = st_flu[pl.ds(c, groups, stride=8), :]
+        force = beta * (f - v)
+        moved = v + drag_step * force / volume
+        st_vel[pl.ds(c, groups, stride=8), :] = jnp.where(leaves, 0.0, moved)
+        hi, lo = parts_of(force)
+        tabs[c] = hi.astype(F32)
+        tabs[4 + c] = lo.astype(F32)
+        moved_t[c] = moved
+        hi, lo = parts_of(force.T)
+        gt_hi[c * LANES:(c + 1) * LANES, :] = hi
+        gt_lo[c * LANES:(c + 1) * LANES, :] = lo
+        hi, lo = parts_of(moved.T)
+        gt_hi[(4 + c) * LANES:(5 + c) * LANES, :] = hi
+        gt_lo[(4 + c) * LANES:(5 + c) * LANES, :] = lo
+    hi, lo = parts_of(volume)
+    tabs[3] = hi.astype(F32)
+    tabs[7] = lo.astype(F32)
+    hi, lo = parts_of(volume.T)
+    gt_hi[3 * LANES:4 * LANES, :] = hi
+    gt_lo[3 * LANES:4 * LANES, :] = lo
+    hgt = height[...].astype(F32)
+    tabs[8] = hgt
+    tabs[9] = jnp.where(leaves, -1.0, row[...].astype(F32))
+    gt_hi[7 * LANES:8 * LANES, :] = hgt.T.astype(BF16)
+
+    def unstage(step, carry):
+        for k in range(8):
+            g = step * 8 + k
+            at = pl.multiple_of(g * LANES, LANES)
+            to = pl.multiple_of(g * 8, 8)
+            kept[:, pl.ds(at, LANES)] = st_vel[pl.ds(to, 3), :]
+        return carry
+
+    lax.fori_loop(0, groups // 8, unstage, 0)
+
+    chunk = 256
+    lane_no = lax.broadcasted_iota(jnp.int32, (LANES, chunk), 0).astype(F32)
+    iota_c = iota16[:, :chunk]
+    for d in range(4):
+        def pick(step, carry):
+            at = pl.multiple_of(step * chunk, chunk)
+            ids = mlist[d:d + 1, pl.ds(at, chunk)]
+            hot = one_hot(spread16((ids // LANES).astype(F32)), groups, iota_c)
+            here = lane_no == (ids % LANES).astype(F32)
+            got = []
+            for f in range(8):
+                part = jnp.dot(gt_hi[f * LANES:(f + 1) * LANES, :], hot, preferred_element_type=F32)
+                if f < 7:
+                    part = part + jnp.dot(
+                        gt_lo[f * LANES:(f + 1) * LANES, :], hot, preferred_element_type=F32
+                    )
+                got.append(jnp.sum(jnp.where(here, part, 0.0), axis=0, keepdims=True))
+            gath[:, pl.ds(at, chunk)] = jnp.concatenate(got, axis=0)
+            return carry
+
+        lax.fori_loop(0, migs // chunk, pick, 0)
+        g8 = gath[...]
+        mov[d] = g8[4:7]
+        h16 = spread16(g8[7:8])
+        hits = [iota16 == h16 - float(16 * block) for block in range(LANES // 16)]
+        pieces = []
+        for f in range(4):
+            pieces.append(parts_of(g8[f:f + 1]))
+        for which in range(2):
+            for f in range(4):
+                v16 = spread16(pieces[f][which].astype(F32))
+                for block in range(LANES // 16):
+                    base = (which * 4 + f) * LANES + block * 16
+                    b0[base:base + 16, :migs] = jnp.where(hits[block], v16, jnp.zeros((), BF16))
+        slot_hot = one_hot(spread16(mslot[d:d + 1, :].astype(F32)), slots, iota16)
+        block_rows = lax.dot_general(slot_hot, b0[:, :migs], NT, preferred_element_type=F32)
+        rows[d, 0:slots, :] = block_rows[:, :4 * LANES] + block_rows[:, 4 * LANES:]
+        rows[d, slots:slots + 1, 0:slots] = side[d:d + 1, :].astype(F32)
+
+    iota_l = iota16[:, :LANES]
+
+    def build(group0, b, a):
+        for k in range(GROUP):
+            g = group0 + k
+            cols = slice(k * LANES, (k + 1) * LANES)
+            h16 = spread16(tabs[8, pl.ds(g, 1), :])
+            r16 = spread16(tabs[9, pl.ds(g, 1), :])
+            hits = [iota_l == h16 - float(16 * block) for block in range(LANES // 16)]
+            for p in range(8):
+                v16 = spread16(tabs[p, pl.ds(g, 1), :])
+                for block in range(LANES // 16):
+                    base = p * LANES + block * 16
+                    b[base:base + 16, cols] = jnp.where(hits[block], v16, jnp.zeros((), BF16))
+            for block in range(row_count // 16):
+                a[block * 16:(block + 1) * 16, cols] = jnp.where(
+                    iota_l == r16 - float(16 * block), jnp.ones((), BF16), jnp.zeros((), BF16)
+                )
+
+    def add(b, a):
+        acc[...] += lax.dot_general(b[...], a[...], NT, preferred_element_type=F32)
+
+    acc[...] = jnp.zeros_like(acc)
+    build(0, b0, a0)
+    pairs = groups // (2 * GROUP)
+
+    def deposit(step, carry):
+        build(step * 2 * GROUP + GROUP, b1, a1)
+        add(b0, a0)
+        build(jnp.minimum(step + 1, pairs - 1) * 2 * GROUP, b0, a0)
+        add(b1, a1)
+        return carry
+
+    lax.fori_loop(0, pairs, deposit, 0)
+    for f in range(4):
+        total = acc[f * LANES:(f + 1) * LANES, :] + acc[(4 + f) * LANES:(5 + f) * LANES, :]
+        dep[f] = total.T
+
+
+def local_part(fibre_vel, fluid_vel, fibre_props, fibre_row, fibre_height, migrant_list, migrant_slot, side_rows, row_count):
+    fibres = fibre_vel.shape[1]
+    groups = fibres // LANES
+    migs = migrant_list.shape[1]
+    slots = side_rows.shape[1]
+    wide = GROUP * LANES
+    vm = pl.BlockSpec(memory_space=pltpu.VMEM)
+    return pl.pallas_call(
+        local_kernel,
+        out_shape=(
+            jax.ShapeDtypeStruct((3, fibres), F32),
+            jax.ShapeDtypeStruct((4, row_count, LANES), F32),
+            jax.ShapeDtypeStruct((4, slots + 8, 4 * LANES), F32),
+            jax.ShapeDtypeStruct((4, 3, migs), F32),
+        ),
+        in_specs=[vm] * 8,
+        out_specs=(vm,) * 4,
+        scratch_shapes=[
+            pltpu.VMEM((groups * 8, LANES), F32),
+            pltpu.VMEM((groups * 8, LANES), F32),
+            pltpu.VMEM((groups * 8, LANES), F32),
+            pltpu.VMEM((10, groups, LANES), F32),
+            pltpu.VMEM((3, groups, LANES), F32),
+            pltpu.VMEM((8 * LANES, groups), BF16),
+            pltpu.VMEM((7 * LANES, groups), BF16),
+            pltpu.VMEM((8, migs), F32),
+            pltpu.VMEM((8 * LANES, wide), BF16),
+            pltpu.VMEM((row_count, wide), BF16),
+            pltpu.VMEM((8 * LANES, wide), BF16),
+            pltpu.VMEM((row_count, wide), BF16),
+            pltpu.VMEM((8 * LANES, row_count), F32),
+        ],
+        compiler_params=pltpu.CompilerParams(vmem_limit_bytes=56 * 1024 * 1024),
+        cost_estimate=pl.CostEstimate(flops=17_000_000_000, bytes_accessed=3_000_000, transcendentals=0),
+        name="fibres",
+    )(
+        fibre_vel, fluid_vel, fibre_props,
+        fibre_row.reshape(groups, LANES), fibre_height.reshape(groups, LANES),
+        migrant_list, migrant_slot, side_rows,
+    )
 
 
 def passed_along(value, axis, steps):
@@ -90,39 +308,19 @@
     row_count = width_x * width_y
     cell_count = row_count * width_z
     slot_count = side_rows.shape[1]
-    fibre_cell = fibre_row * width_z + fibre_height
-    partials, moved_vel = fibre_terms(fibre_vel, fluid_vel, fibre_props)
-    staying = jnp.ones((fibre_vel.shape[1],), jnp.float32).at[migrant_list.reshape(-1)].set(0.0)
-    kept_fibres = moved_vel * staying[None, :]
-    deposit = (
-        jnp.zeros((4, cell_count), jnp.float32).at[:, fibre_cell].add(partials * staying[None, :])
+    kept_fibres, deposit, rows, movers = local_part(
+        fibre_vel, fluid_vel, fibre_props, fibre_row, fibre_height,
+        migrant_list, migrant_slot, side_rows, row_count,
     )
     arrived = []
     for direction in range(4):
-        chosen = migrant_list[direction]
-        fibre_heights = fibre_height[chosen]
         step_by = 1 if direction % 2 == 1 else -1
-        slot_cells = migrant_slot[direction] * width_z + fibre_heights
-        row_block = (
-            jnp.zeros((4, slot_count * width_z), jnp.float32)
-            .at[:, slot_cells]
-            .add(partials[:, chosen])
+        got_rows, got_vel = passed_along(
+            (rows[direction], movers[direction]), "gx" if direction < 2 else "gy", step_by
         )
-        row_block = row_block.reshape(4, slot_count, width_z)
-        if direction < 2:
-            got_rows, got_ids, got_vel = passed_along(
-                (row_block, side_rows[direction], moved_vel[:, chosen]), "gx", step_by
-            )
-        else:
-            got_rows, got_ids, got_vel = passed_along(
-                (row_block, side_rows[direction], moved_vel[:, chosen]), "gy", step_by
-            )
-        deposit = (
-            deposit.reshape(4, row_count, width_z)
-            .at[:, got_ids]
-            .add(got_rows)
-            .reshape(4, cell_count)
-        )
+        got_ids = got_rows[slot_count, :slot_count].astype(jnp.int32)
+        moved_rows = got_rows[:slot_count].reshape(slot_count, 4, width_z).transpose(1, 0, 2)
+        deposit = deposit.at[:, got_ids].add(moved_rows)
         arrived.append(got_vel)
     drag_field = deposit[0:3].reshape(3, width_x, width_y, width_z)
     void_fraction = 1.0 / (1.0 + deposit[3].reshape(width_x, width_y, width_z))

time: 549 us -> 155 us (0.28); the launches traced: 540 us -> 155 us
  other arithmetic: 324 us -> 30.1 us
  local copies, waits for them, and re-layouts: 166 us -> 41.6 us
  Pallas kernels: 0 us -> 36.9 us
  starting transfers between devices: 38.6 us -> 32.3 us
    scatter-add x9 -> x4, other arithmetic: 251 us -> 4.36 us  [body(): deposit = deposit.at[:, got_ids].add(moved_rows)]
    gather x8 -> x0, local copies, waits for them, and re-layouts: 62.2 us -> none  [the longest x4 37.8 us: body(): moved_vel[:, chosen]]
    pallas_call x0 -> x1, Pallas kernels: none -> 36.9 us  [local_part(): pl.pallas_call(local_kernel, out_shape=(jax.ShapeDtypeStruct((3, fibres),...]
    unnamed x87 -> x65, local copies, waits for them, and re-layouts: 37.9 us -> 2.92 us
    mul x1 -> x0, other arithmetic: 28.4 us -> none  [body(): kept_fibres = moved_vel * staying[None, :]]
    concatenate x1 -> x0, other arithmetic: 17.3 us -> none  [fibre_terms(): partials = jnp.concatenate([drag_force, volume], axis=0)]
    scatter x1 -> x0, local copies, waits for them, and re-layouts: 15.6 us -> none  [body(): jnp.ones((fibre_vel.shape[1],), jnp.float32).at[migrant_list.reshape(-1)]]
    reshape x5 -> x4, local copies, waits for them, and re-layouts: 10.7 us -> 0.07 us  [body(): got_rows[:slot_count].reshape(slot_count, 4, width_z).transpose(1, 0, 2)]
  transfers between devices with their start and end apart: 30 -> 26, of which waited for: 8 -> 10; matrix products, arithmetic and copies ran while one was open for 83% -> 23% of each run, Pallas kernels for 0% -> 0%
where the time goes in v1:
time: 155 us
  local copies, waits for them, and re-layouts  41.6 us (27%)
  Pallas kernels  36.9 us (24%)
  starting transfers between devices  32.3 us (21%)
  other arithmetic  30.1 us (19%)
  waiting for transfers between devices  12.4 us (8%)
    pallas_call x1, Pallas kernels, local_part(): pl.pallas_call(local_kernel, out_shape=(jax.ShapeDtypeStruct((3, fibres),...  36.9 us
    concatenate x6, other arithmetic, padded(): array = jnp.concatenate([before, array, after], axis=dim)  17.9 us
    concatenate x6, local copies, waits for them, and re-layouts, padded(): array = jnp.concatenate([before, array, after], axis=dim)  14.2 us
    ppermute x9, starting transfers between devices, padded(): after = lax.ppermute(leading, axis, down)  13.2 us
    ppermute x8, starting transfers between devices, passed_along(): return lax.ppermute(value, axis, pairs)  12.2 us
    ppermute x6, local copies, waits for them, and re-layouts, padded(): after = lax.ppermute(leading, axis, down)  10.2 us
    ppermute x6, local copies, waits for them, and re-layouts, padded(): before = lax.ppermute(last, axis, up)  10 us
    ppermute x9, starting transfers between devices, padded(): before = lax.ppermute(last, axis, up)  6.9 us
  transfers between devices with their start and end apart: 26, of which 10 were waited for; matrix products, arithmetic and copies ran while one was open for 23% of the time, Pallas kernels for 0%

profile of v1, /device:TPU:0, one launch (start us, length us, event | category | flops | bytes accessed | tf_op | source)
XLA Modules:
  0.0 154.6 jit_solution(14139137303051028016)
XLA Ops:
  0.6 36.9 %fibres.1 = (f32[3,32768]{1,0:T(4,128)}, f32[4,256,128]{2,1,0:T(8,128)}, f32[4,24,512]{2,1,0:T(8,128)}, f32[4,3,1024]{2,1,0:T(4,128)}) custom-call(f32[3,32768]{1,0:T(4,128)} %vel.1, f32[3,32768]{1,0:T(4,128)} %flu.1, f32[2,32768]{1,0:T(2,128)} %prop.1, s32[256,128]{1,0:T(8,128)} %bitcast.58, s32[256,128]{1,0:T(8,128)} %bitcast.59, s32[4,1024]{1,0:T(4,128)} %mlist.1, ...), custom_call_target="tpu_custom_call" | custom-call | flops 16999999488 | bytes 3000000 | tf_op jit(solution)/shard_map/fibres/pallas_call | solution.py:197
  37.6 0.9 slice_bitcast_fusion
  38.9 4.1 %collective-permute-start.2 = (f32[24,512]{1,0:T(8,128)S(1)}, f32[24,512]{1,0:T(8,128)S(1)}, u32[]{:S(2)}, u32[]{:S(2)}) collective-permute-start(f32[24,512]{1,0:T(8,128)S(1)} %get-tuple-element.51), channel_id=1, source_target_pairs={{0,14},{2,0},{4,2},{6,4},{8,6},{10,8},{12,10},{14,12},{1,15},{3,1}... | collective-permute-start | bytes 147464 | tf_op jit(solution)/shard_map/ppermute | solution.py:235
  43.1 1.9 %collective-permute-start.1 = (f32[24,512]{1,0:T(8,128)S(1)}, f32[24,512]{1,0:T(8,128)S(1)}, u32[]{:S(2)}, u32[]{:S(2)}) collective-permute-start(f32[24,512]{1,0:T(8,128)S(1)} %get-tuple-element.52), channel_id=1, source_target_pairs={{0,16},{16,0},{1,17},{17,1},{2,18},{18,2},{3,19},{19,3},{4,20},{20... | collective-permute-start | bytes 147464 | tf_op jit(solution)/shard_map/ppermute | solution.py:235
  45.1 1.4 copy.50
  46.6 0.6 collective-permute-done.1
  47.2 1.9 %collective-permute-done = f32[24,512]{1,0:T(8,128)S(1)} collective-permute-done((f32[24,512]{1,0:T(8,128)S(1)}, f32[24,512]{1,0:T(8,128)S(1)}, u32[]{:S(2)}, u32[]{:S(2)}) %collective-permute-start) | collective-permute-done | bytes 49184 | tf_op jit(solution)/shard_map/ppermute | solution.py:235
  49.1 1.1 scatter_fusion
  50.2 1.1 scatter_fusion.1
  51.3 1.1 scatter_fusion.2
  52.4 1.1 scatter_fusion.3
  53.8 0.6 collective-permute-start.4
  54.4 1.5 collective-permute-start.5
  55.9 2.2 %collective-permute-done.4 = f32[4,1,32,128]{3,2,1,0:T(8,128)S(1)} collective-permute-done((f32[4,1,32,128]{3,2,1,0:T(8,128)S(1)}, f32[4,1,32,128]{3,2,1,0:T(8,128)S(1)}, u32[]{:S(2)}, u32[]{:S(2)}) %collective-permute-start.4) | collective-permute-done | bytes 65568 | tf_op jit(solution)/shard_map/ppermute | solution.py:245
  58.1 0.7 collective-permute-done.5
  59.0 3.5 %collective-permute-start.7 = (f32[4,10,1,128]{3,1,2,0:T(8,128)S(1)}, f32[4,10,1,128]{3,1,2,0:T(8,128)S(1)}, u32[]{:S(2)}, u32[]{:S(2)}) collective-permute-start(f32[4,10,1,128]{3,1,2,0:T(8,128)S(1)} %copy.78), channel_id=1, source_target_pairs={{2,0},{4,2},{6,4},{8,6},{10,8},{12,10},{14,12},{0,14},{3,1},{5,3},... | collective-permute-start | bytes 61448 | tf_op jit(solution)/shard_map/ppermute | solution.py:246
  62.5 2.9 %copy.55 = f32[4,10,32,128]{2,1,3,0:T(8,128)} copy(f32[4,10,32,128]{3,2,1,0:T(8,128)S(1)} %pad_maximum_fusion.5) | data formatting | bytes 1310720 | tf_op jit(solution)/shard_map/concatenate | solution.py:247
  65.5 3.0 %copy.54 = f32[4,10,1,128]{2,1,3,0:T(8,128)} copy(f32[4,10,1,128]{3,1,2,0:T(8,128)S(1)} %collective-permute-done.6) | data formatting | bytes 40960 | tf_op jit(solution)/shard_map/ppermute | solution.py:245
  68.4 2.9 %copy.56 = f32[4,10,1,128]{2,1,3,0:T(8,128)} copy(f32[4,10,1,128]{3,1,2,0:T(8,128)S(1)} %collective-permute-done.7) | data formatting | bytes 40960 | tf_op jit(solution)/shard_map/ppermute | solution.py:246
  71.3 6.9 %pad_maximum_fusion = f32[4,10,34,128]{2,1,3,0:T(8,128)S(1)} fusion(f32[4,10,1,128]{2,1,3,0:T(8,128)} %copy.56, f32[4,10,32,128]{2,1,3,0:T(8,128)} %copy.55, f32[4,10,1,128]{2,1,3,0:T(8,128)} %copy.54), kind=kLoop, calls=%fused_computation.4 | loop fusion | flops 348160 | bytes 1392640 | tf_op jit(solution)/shard_map/concatenate | solution.py:247
  78.2 2.0 %copy-done = f32[4,10,34,128]{2,1,3,0:T(8,128)} copy-done((f32[4,10,34,128]{2,1,3,0:T(8,128)}, f32[4,10,34,128]{2,1,3,0:T(8,128)S(1)}, u32[]{:S(2)}) %copy-start) | copy-done | bytes 696344
  80.2 1.5 collective-permute-start.8
  82.3 2.7 %copy.58 = f32[4,10,34,128]{3,2,1,0:T(8,128)S(1)} copy(f32[4,10,34,128]{2,1,3,0:T(8,128)} %copy-done) | data formatting | bytes 1392640 | tf_op jit(solution)/shard_map/concatenate | solution.py:247
  85.0 0.7 collective-permute-done.9
  87.8 0.6 fusion.18
  88.4 1.4 collective-permute-start.10
  89.7 0.7 collective-permute-start.11
  90.4 2.1 %collective-permute-done.10 = f32[3,1,32,128]{3,2,1,0:T(8,128)S(1)} collective-permute-done((f32[3,1,32,128]{3,2,1,0:T(8,128)S(1)}, f32[3,1,32,128]{3,2,1,0:T(8,128)S(1)}, u32[]{:S(2)}, u32[]{:S(2)}) %collective-permute-start.10) | collective-permute-done | bytes 49184 | tf_op jit(solution)/shard_map/ppermute | solution.py:245
  92.5 1.3 collective-permute-done.11
  94.1 3.5 %collective-permute-start.13 = (f32[3,10,1,128]{3,1,2,0:T(8,128)S(1)}, f32[3,10,1,128]{3,1,2,0:T(8,128)S(1)}, u32[]{:S(2)}, u32[]{:S(2)}) collective-permute-start(f32[3,10,1,128]{3,1,2,0:T(8,128)S(1)} %copy.80), channel_id=1, source_target_pairs={{2,0},{4,2},{6,4},{8,6},{10,8},{12,10},{14,12},{0,14},{3,1},{5,3},... | collective-permute-start | bytes 46088 | tf_op jit(solution)/shard_map/ppermute | solution.py:246
  97.6 2.3 %copy.63 = f32[3,10,32,128]{2,1,3,0:T(8,128)} copy(f32[3,10,32,128]{3,2,1,0:T(8,128)S(1)} %pad_maximum_fusion.6) | data formatting | bytes 983040 | tf_op jit(solution)/shard_map/concatenate | solution.py:247
  99.9 2.3 %copy.62 = f32[3,10,1,128]{2,1,3,0:T(8,128)} copy(f32[3,10,1,128]{3,1,2,0:T(8,128)S(1)} %collective-permute-done.12) | data formatting | bytes 30720 | tf_op jit(solution)/shard_map/ppermute | solution.py:245
  102.2 2.2 %copy.64 = f32[3,10,1,128]{2,1,3,0:T(8,128)} copy(f32[3,10,1,128]{3,1,2,0:T(8,128)S(1)} %collective-permute-done.13) | data formatting | bytes 30720 | tf_op jit(solution)/shard_map/ppermute | solution.py:246
  104.4 5.4 %pad_maximum_fusion.1 = f32[3,10,34,128]{2,1,3,0:T(8,128)S(1)} fusion(f32[3,10,1,128]{2,1,3,0:T(8,128)} %copy.64, f32[3,10,32,128]{2,1,3,0:T(8,128)} %copy.63, f32[3,10,1,128]{2,1,3,0:T(8,128)} %copy.62), kind=kLoop, calls=%fused_computation.5 | loop fusion | flops 261120 | bytes 1044480 | tf_op jit(solution)/shard_map/concatenate | solution.py:247
  109.9 0.6 fusion.46
  110.5 0.9 collective-permute-start.15
  111.4 1.2 collective-permute-start.14
  112.5 1.9 %copy.66 = f32[3,10,34,128]{3,2,1,0:T(8,128)} copy(f32[3,10,34,128]{2,1,3,0:T(8,128)S(1)} %pad_maximum_fusion.1) | data formatting | bytes 1044480 | tf_op jit(solution)/shard_map/concatenate | solution.py:247
  114.6 1.2 copy.67
  115.9 1.1 copy.65
  117.0 1.6 %maximum_select_fusion = f32[3,10,34,130]{3,2,1,0:T(8,128)S(1)} fusion(f32[3,10,34,1]{3,2,1,0:T(8,128)S(1)} %copy.67, f32[3,10,34,128]{3,2,1,0:T(8,128)} %copy.66, f32[3,10,34,1]{3,2,1,0:T(8,128)S(1)} %copy.65, pred[130]{0:T(512)(128)(4,1)S(1)} %compare_or_fusion), kind=kLoop, calls=%fused_computation.10 | loop fusion | flops 397800 | bytes 1060930 | tf_op jit(solution)/shard_map/jit(_where)/select_n | solution.py:341
  118.7 0.6 fusion.11
  119.3 0.8 collective-permute-start.16
  120.1 1.3 collective-permute-start.17
  121.4 2.1 %collective-permute-done.16 = f32[3,1,32,128]{3,2,1,0:T(8,128)S(1)} collective-permute-done((f32[3,1,32,128]{3,2,1,0:T(8,128)S(1)}, f32[3,1,32,128]{3,2,1,0:T(8,128)S(1)}, u32[]{:S(2)}, u32[]{:S(2)}) %collective-permute-start.16) | collective-permute-done | bytes 49184 | tf_op jit(solution)/shard_map/ppermute | solution.py:245
  123.5 0.7 collective-permute-done.17
  124.8 0.6 slice_bitcast_fusion.7
  125.4 1.3 collective-permute-start.22
  126.8 3.5 %collective-permute-start.24 = (f32[3,1024]{1,0:T(4,128)}, f32[3,1024]{1,0:T(4,128)}, u32[]{:S(2)}, u32[]{:S(2)}) collective-permute-start(f32[3,1024]{1,0:T(4,128)} %get-tuple-element.56), channel_id=1, source_target_pairs={{0,14},{2,0},{4,2},{6,4},{8,6},{10,8},{12,10},{14,12},{1,15},{3,1}... | collective-permute-start | bytes 36872 | tf_op jit(solution)/shard_map/ppermute | solution.py:235
  130.3 2.3 %copy.71 = f32[3,10,32,128]{2,1,3,0:T(8,128)} copy(f32[3,10,32,128]{3,2,1,0:T(8,128)S(1)} %pad_maximum_fusion.7) | data formatting | bytes 983040 | tf_op jit(solution)/shard_map/concatenate | solution.py:247
  132.6 0.7 collective-permute-start.23
  133.3 2.3 %copy.70 = f32[3,10,1,128]{2,1,3,0:T(8,128)} copy(f32[3,10,1,128]{3,1,2,0:T(8,128)S(1)} %collective-permute-done.18) | data formatting | bytes 30720 | tf_op jit(solution)/shard_map/ppermute | solution.py:245
  135.6 2.2 %copy.72 = f32[3,10,1,128]{2,1,3,0:T(8,128)} copy(f32[3,10,1,128]{3,1,2,0:T(8,128)S(1)} %collective-permute-done.19) | data formatting | bytes 30720 | tf_op jit(solution)/shard_map/ppermute | solution.py:246
  137.8 5.4 %pad_maximum_fusion.2 = f32[3,10,34,128]{2,1,3,0:T(8,128)S(1)} fusion(f32[3,10,1,128]{2,1,3,0:T(8,128)} %copy.72, f32[3,10,32,128]{2,1,3,0:T(8,128)} %copy.71, f32[3,10,1,128]{2,1,3,0:T(8,128)} %copy.70), kind=kLoop, calls=%fused_computation.6 | loop fusion | flops 261120 | bytes 1044480 | tf_op jit(solution)/shard_map/concatenate | solution.py:247
  143.3 0.6 fusion.45
  143.9 0.9 collective-permute-start.20
  144.8 1.2 collective-permute-start.21
  145.9 0.8 pad_maximum_fusion.10
  146.7 0.7 copy.76
  147.4 1.9 %copy.74 = f32[3,10,34,128]{3,2,1,0:T(8,128)} copy(f32[3,10,34,128]{2,1,3,0:T(8,128)S(1)} %pad_maximum_fusion.2) | data formatting | bytes 1044480 | tf_op jit(solution)/shard_map/concatenate | solution.py:247
  149.4 1.1 copy.75
  150.5 1.1 copy.73
  151.6 1.6 %maximum_select_fusion.1 = f32[3,10,34,130]{3,2,1,0:T(8,128)S(1)} fusion(f32[3,10,34,1]{3,2,1,0:T(8,128)S(1)} %copy.75, f32[3,10,34,128]{3,2,1,0:T(8,128)} %copy.74, f32[3,10,34,1]{3,2,1,0:T(8,128)S(1)} %copy.73, pred[130]{0:T(512)(128)(4,1)} %copy-done.28), kind=kLoop, calls=%fused_computation.11 | loop fusion | flops 397800 | bytes 1060930 | tf_op jit(solution)/shard_map/jit(_where)/select_n | solution.py:341
  153.3 1.4 fusion.4
  (117 shorter events, 4.6 us)
Async XLA Ops:
  0.6 53.1 %copy-start.1 = (f32[3,8,32,128]{3,2,1,0:T(8,128)S(1)}, f32[3,8,32,128]{3,2,1,0:T(8,128)}, u32[]{:S(2)}) copy-start(f32[3,8,32,128]{3,2,1,0:T(8,128)} %param.9) | copy-start | bytes 1179652
  38.5 8.0 %collective-permute-start.3 = (f32[24,512]{1,0:T(8,128)S(1)}, f32[24,512]{1,0:T(8,128)S(1)}, u32[]{:S(2)}, u32[]{:S(2)}) collective-permute-start(f32[24,512]{1,0:T(8,128)S(1)} %get-tuple-element.50), channel_id=1, source_target_pairs={{0,2},{2,4},{4,6},{6,8},{8,10},{10,12},{12,14},{14,0},{1,3},{3,5},... | collective-permute-start | bytes 147464 | tf_op jit(solution)/shard_map/ppermute | solution.py:235
  38.9 7.6 %collective-permute-start.2 = (f32[24,512]{1,0:T(8,128)S(1)}, f32[24,512]{1,0:T(8,128)S(1)}, u32[]{:S(2)}, u32[]{:S(2)}) collective-permute-start(f32[24,512]{1,0:T(8,128)S(1)} %get-tuple-element.51), channel_id=1, source_target_pairs={{0,14},{2,0},{4,2},{6,4},{8,6},{10,8},{12,10},{14,12},{1,15},{3,1}... | collective-permute-start | bytes 147464 | tf_op jit(solution)/shard_map/ppermute | solution.py:235
  43.1 4.1 %collective-permute-start.1 = (f32[24,512]{1,0:T(8,128)S(1)}, f32[24,512]{1,0:T(8,128)S(1)}, u32[]{:S(2)}, u32[]{:S(2)}) collective-permute-start(f32[24,512]{1,0:T(8,128)S(1)} %get-tuple-element.52), channel_id=1, source_target_pairs={{0,16},{16,0},{1,17},{17,1},{2,18},{18,2},{3,19},{19,3},{4,20},{20... | collective-permute-start | bytes 147464 | tf_op jit(solution)/shard_map/ppermute | solution.py:235
  45.0 4.1 %collective-permute-start = (f32[24,512]{1,0:T(8,128)S(1)}, f32[24,512]{1,0:T(8,128)S(1)}, u32[]{:S(2)}, u32[]{:S(2)}) collective-permute-start(f32[24,512]{1,0:T(8,128)S(1)} %get-tuple-element.53), channel_id=1, source_target_pairs={{0,16},{16,0},{1,17},{17,1},{2,18},{18,2},{3,19},{19,3},{4,20},{20... | collective-permute-start | bytes 147464 | tf_op jit(solution)/shard_map/ppermute | solution.py:235
  53.5 11.9 %copy-start.2 = (f32[4,256,128]{2,0,1:T(4,128)}, f32[4,256,128]{2,0,1:T(4,128)S(1)}, u32[]{:S(2)}) copy-start(f32[4,256,128]{2,0,1:T(4,128)S(1)} %scatter_fusion.3) | copy-start | bytes 1572868
  53.7 11.7 %copy-start.25 = (f32[1,256,128]{2,0,1:T(1,128)}, f32[1,256,128]{2,0,1:T(1,128)S(1)}, u32[]{:S(2)}) copy-start(f32[1,256,128]{2,0,1:T(1,128)S(1)} %fusion.29) | copy-start | bytes 393220
  53.8 4.3 %collective-permute-start.4 = (f32[4,1,32,128]{3,2,1,0:T(8,128)S(1)}, f32[4,1,32,128]{3,2,1,0:T(8,128)S(1)}, u32[]{:S(2)}, u32[]{:S(2)}) collective-permute-start(f32[4,1,32,128]{3,2,1,0:T(8,128)S(1)} %get-tuple-element.40), channel_id=1, source_target_pairs={{0,16},{16,0},{1,17},{17,1},{2,18},{18,2},{3,19},{19,3},{4,20},{20... | collective-permute-start | bytes 196616 | tf_op jit(solution)/shard_map/ppermute | solution.py:245
  54.4 4.4 %collective-permute-start.5 = (f32[4,1,32,128]{3,2,1,0:T(8,128)S(1)}, f32[4,1,32,128]{3,2,1,0:T(8,128)S(1)}, u32[]{:S(2)}, u32[]{:S(2)}) collective-permute-start(f32[4,1,32,128]{3,2,1,0:T(8,128)S(1)} %get-tuple-element.41), channel_id=1, source_target_pairs={{16,0},{0,16},{17,1},{1,17},{18,2},{2,18},{19,3},{3,19},{20,4},{4,... | collective-permute-start | bytes 196616 | tf_op jit(solution)/shard_map/ppermute | solution.py:246
  58.9 6.5 %collective-permute-start.6 = (f32[4,10,1,128]{3,1,2,0:T(8,128)S(1)}, f32[4,10,1,128]{3,1,2,0:T(8,128)S(1)}, u32[]{:S(2)}, u32[]{:S(2)}) collective-permute-start(f32[4,10,1,128]{3,1,2,0:T(8,128)S(1)} %copy.77), channel_id=1, source_target_pairs={{0,2},{2,4},{4,6},{6,8},{8,10},{10,12},{12,14},{14,0},{1,3},{3,5},... | collective-permute-start | bytes 61448 | tf_op jit(solution)/shard_map/ppermute | solution.py:245
  59.0 9.4 %collective-permute-start.7 = (f32[4,10,1,128]{3,1,2,0:T(8,128)S(1)}, f32[4,10,1,128]{3,1,2,0:T(8,128)S(1)}, u32[]{:S(2)}, u32[]{:S(2)}) collective-permute-start(f32[4,10,1,128]{3,1,2,0:T(8,128)S(1)} %copy.78), channel_id=1, source_target_pairs={{2,0},{4,2},{6,4},{8,6},{10,8},{12,10},{14,12},{0,14},{3,1},{5,3},... | collective-permute-start | bytes 61448 | tf_op jit(solution)/shard_map/ppermute | solution.py:246
  78.2 2.0 %copy-start = (f32[4,10,34,128]{2,1,3,0:T(8,128)}, f32[4,10,34,128]{2,1,3,0:T(8,128)S(1)}, u32[]{:S(2)}) copy-start(f32[4,10,34,128]{2,1,3,0:T(8,128)S(1)} %pad_maximum_fusion) | copy-start | bytes 2088964
  80.2 5.8 %collective-permute-start.8 = (f32[4,10,34,1]{2,1,3,0:T(8,128)S(1)}, f32[4,10,34,1]{2,1,3,0:T(8,128)S(1)}, u32[]{:S(2)}, u32[]{:S(2)}) collective-permute-start(f32[4,10,34,1]{2,1,3,0:T(8,128)S(1)} %get-tuple-element.32), channel_id=1, source_target_pairs={{0,1},{1,0},{2,3},{3,2},{4,5},{5,4},{6,7},{7,6},{8,9},{9,8},{10,11... | collective-permute-start | bytes 16328 | tf_op jit(solution)/shard_map/ppermute | solution.py:245
  81.7 3.9 %collective-permute-start.9 = (f32[4,10,34,1]{2,1,3,0:T(8,128)S(1)}, f32[4,10,34,1]{2,1,3,0:T(8,128)S(1)}, u32[]{:S(2)}, u32[]{:S(2)}) collective-permute-start(f32[4,10,34,1]{2,1,3,0:T(8,128)S(1)} %get-tuple-element.33), channel_id=1, source_target_pairs={{1,0},{0,1},{3,2},{2,3},{5,4},{4,5},{7,6},{6,7},{9,8},{8,9},{11,10... | collective-permute-start | bytes 16328 | tf_op jit(solution)/shard_map/ppermute | solution.py:246
  82.3 34.7 %copy-start.28 = (pred[130]{0:T(512)(128)(4,1)}, pred[130]{0:T(512)(128)(4,1)S(1)}, u32[]{:S(2)}) copy-start(pred[130]{0:T(512)(128)(4,1)S(1)} %compare_or_fusion) | copy-start | bytes 394
  86.7 1.0 copy-start.3
  86.7 1.1 copy-start.26
  87.5 6.3 %copy-start.4 = (f32[8,32,128]{2,1,0:T(8,128)}, f32[8,32,128]{2,1,0:T(8,128)S(1)}, u32[]{:S(2)}) copy-start(f32[8,32,128]{2,1,0:T(8,128)S(1)} %get-tuple-element.25) | copy-start | bytes 393220
  87.6 6.3 %copy-start.7 = (f32[8,32,128]{2,1,0:T(8,128)}, f32[8,32,128]{2,1,0:T(8,128)S(1)}, u32[]{:S(2)}) copy-start(f32[8,32,128]{2,1,0:T(8,128)S(1)} %get-tuple-element.26) | copy-start | bytes 393220
  87.6 6.3 %copy-start.10 = (f32[8,32,128]{2,1,0:T(8,128)}, f32[8,32,128]{2,1,0:T(8,128)S(1)}, u32[]{:S(2)}) copy-start(f32[8,32,128]{2,1,0:T(8,128)S(1)} %get-tuple-element.27) | copy-start | bytes 393220
  87.6 6.3 %copy-start.13 = (f32[8,32,128]{2,1,0:T(8,128)}, f32[8,32,128]{2,1,0:T(8,128)S(1)}, u32[]{:S(2)}) copy-start(f32[8,32,128]{2,1,0:T(8,128)S(1)} %get-tuple-element.28) | copy-start | bytes 393220
  87.6 6.3 %copy-start.16 = (f32[8,32,128]{2,1,0:T(8,128)}, f32[8,32,128]{2,1,0:T(8,128)S(1)}, u32[]{:S(2)}) copy-start(f32[8,32,128]{2,1,0:T(8,128)S(1)} %get-tuple-element.29) | copy-start | bytes 393220
  87.6 6.3 %copy-start.19 = (f32[8,32,128]{2,1,0:T(8,128)}, f32[8,32,128]{2,1,0:T(8,128)S(1)}, u32[]{:S(2)}) copy-start(f32[8,32,128]{2,1,0:T(8,128)S(1)} %get-tuple-element.30) | copy-start | bytes 393220
  87.6 6.3 %copy-start.22 = (f32[8,32,128]{2,1,0:T(8,128)}, f32[8,32,128]{2,1,0:T(8,128)S(1)}, u32[]{:S(2)}) copy-start(f32[8,32,128]{2,1,0:T(8,128)S(1)} %get-tuple-element.31) | copy-start | bytes 393220
  88.4 4.2 %collective-permute-start.10 = (f32[3,1,32,128]{3,2,1,0:T(8,128)S(1)}, f32[3,1,32,128]{3,2,1,0:T(8,128)S(1)}, u32[]{:S(2)}, u32[]{:S(2)}) collective-permute-start(f32[3,1,32,128]{3,2,1,0:T(8,128)S(1)} %get-tuple-element.48), channel_id=1, source_target_pairs={{0,16},{16,0},{1,17},{17,1},{2,18},{18,2},{3,19},{19,3},{4,20},{20... | collective-permute-start | bytes 147464 | tf_op jit(solution)/shard_map/ppermute | solution.py:245
  89.7 4.1 %collective-permute-start.11 = (f32[3,1,32,128]{3,2,1,0:T(8,128)S(1)}, f32[3,1,32,128]{3,2,1,0:T(8,128)S(1)}, u32[]{:S(2)}, u32[]{:S(2)}) collective-permute-start(f32[3,1,32,128]{3,2,1,0:T(8,128)S(1)} %get-tuple-element.49), channel_id=1, source_target_pairs={{16,0},{0,16},{17,1},{1,17},{18,2},{2,18},{19,3},{3,19},{20,4},{4,... | collective-permute-start | bytes 147464 | tf_op jit(solution)/shard_map/ppermute | solution.py:246
  94.0 5.9 %collective-permute-start.12 = (f32[3,10,1,128]{3,1,2,0:T(8,128)S(1)}, f32[3,10,1,128]{3,1,2,0:T(8,128)S(1)}, u32[]{:S(2)}, u32[]{:S(2)}) collective-permute-start(f32[3,10,1,128]{3,1,2,0:T(8,128)S(1)} %copy.79), channel_id=1, source_target_pairs={{0,2},{2,4},{4,6},{6,8},{8,10},{10,12},{12,14},{14,0},{1,3},{3,5},... | collective-permute-start | bytes 46088 | tf_op jit(solution)/shard_map/ppermute | solution.py:245
  94.1 8.1 %collective-permute-start.13 = (f32[3,10,1,128]{3,1,2,0:T(8,128)S(1)}, f32[3,10,1,128]{3,1,2,0:T(8,128)S(1)}, u32[]{:S(2)}, u32[]{:S(2)}) collective-permute-start(f32[3,10,1,128]{3,1,2,0:T(8,128)S(1)} %copy.80), channel_id=1, source_target_pairs={{2,0},{4,2},{6,4},{8,6},{10,8},{12,10},{14,12},{0,14},{3,1},{5,3},... | collective-permute-start | bytes 46088 | tf_op jit(solution)/shard_map/ppermute | solution.py:246
  110.5 4.1 %collective-permute-start.15 = (f32[3,10,34,1]{2,1,3,0:T(8,128)}, f32[3,10,34,1]{2,1,3,0:T(8,128)}, u32[]{:S(2)}, u32[]{:S(2)}) collective-permute-start(f32[3,10,34,1]{2,1,3,0:T(8,128)} %get-tuple-element.37), channel_id=1, source_target_pairs={{1,0},{0,1},{3,2},{2,3},{5,4},{4,5},{7,6},{6,7},{9,8},{8,9},{11,10... | collective-permute-start | bytes 12248 | tf_op jit(solution)/shard_map/ppermute | solution.py:246
  111.4 4.5 %collective-permute-start.14 = (f32[3,10,34,1]{2,1,3,0:T(8,128)}, f32[3,10,34,1]{2,1,3,0:T(8,128)}, u32[]{:S(2)}, u32[]{:S(2)}) collective-permute-start(f32[3,10,34,1]{2,1,3,0:T(8,128)} %get-tuple-element.36), channel_id=1, source_target_pairs={{0,1},{1,0},{2,3},{3,2},{4,5},{5,4},{6,7},{7,6},{8,9},{9,8},{10,11... | collective-permute-start | bytes 12248 | tf_op jit(solution)/shard_map/ppermute | solution.py:245
  114.5 4.1 %copy-start.5 = (f32[8,32,128]{2,1,0:T(8,128)S(1)}, f32[8,32,128]{2,1,0:T(8,128)}, u32[]{:S(2)}) copy-start(f32[8,32,128]{2,1,0:T(8,128)} %copy-done.4) | copy-start | bytes 393220
  114.5 4.2 %copy-start.8 = (f32[8,32,128]{2,1,0:T(8,128)S(1)}, f32[8,32,128]{2,1,0:T(8,128)}, u32[]{:S(2)}) copy-start(f32[8,32,128]{2,1,0:T(8,128)} %copy-done.7) | copy-start | bytes 393220
  114.5 4.2 %copy-start.11 = (f32[8,32,128]{2,1,0:T(8,128)S(1)}, f32[8,32,128]{2,1,0:T(8,128)}, u32[]{:S(2)}) copy-start(f32[8,32,128]{2,1,0:T(8,128)} %copy-done.10) | copy-start | bytes 393220
  114.5 4.2 %copy-start.14 = (f32[8,32,128]{2,1,0:T(8,128)S(1)}, f32[8,32,128]{2,1,0:T(8,128)}, u32[]{:S(2)}) copy-start(f32[8,32,128]{2,1,0:T(8,128)} %copy-done.13) | copy-start | bytes 393220
  114.5 4.2 %copy-start.17 = (f32[8,32,128]{2,1,0:T(8,128)S(1)}, f32[8,32,128]{2,1,0:T(8,128)}, u32[]{:S(2)}) copy-start(f32[8,32,128]{2,1,0:T(8,128)} %copy-done.16) | copy-start | bytes 393220
  114.5 4.2 %copy-start.20 = (f32[8,32,128]{2,1,0:T(8,128)S(1)}, f32[8,32,128]{2,1,0:T(8,128)}, u32[]{:S(2)}) copy-start(f32[8,32,128]{2,1,0:T(8,128)} %copy-done.19) | copy-start | bytes 393220
  114.5 4.2 %copy-start.23 = (f32[8,32,128]{2,1,0:T(8,128)S(1)}, f32[8,32,128]{2,1,0:T(8,128)}, u32[]{:S(2)}) copy-start(f32[8,32,128]{2,1,0:T(8,128)} %copy-done.22) | copy-start | bytes 393220
  118.6 6.2 %copy-start.27 = (f32[4,3,1024]{2,1,0:T(4,128)S(1)}, f32[4,3,1024]{2,1,0:T(4,128)}, u32[]{:S(2)}) copy-start(f32[4,3,1024]{2,1,0:T(4,128)} %get-tuple-element.10) | copy-start | bytes 147460
  119.3 4.2 %collective-permute-start.16 = (f32[3,1,32,128]{3,2,1,0:T(8,128)S(1)}, f32[3,1,32,128]{3,2,1,0:T(8,128)S(1)}, u32[]{:S(2)}, u32[]{:S(2)}) collective-permute-start(f32[3,1,32,128]{3,2,1,0:T(8,128)S(1)} %get-tuple-element.46), channel_id=1, source_target_pairs={{0,16},{16,0},{1,17},{17,1},{2,18},{18,2},{3,19},{19,3},{4,20},{20... | collective-permute-start | bytes 147464 | tf_op jit(solution)/shard_map/ppermute | solution.py:245
  120.1 4.1 %collective-permute-start.17 = (f32[3,1,32,128]{3,2,1,0:T(8,128)S(1)}, f32[3,1,32,128]{3,2,1,0:T(8,128)S(1)}, u32[]{:S(2)}, u32[]{:S(2)}) collective-permute-start(f32[3,1,32,128]{3,2,1,0:T(8,128)S(1)} %get-tuple-element.47), channel_id=1, source_target_pairs={{16,0},{0,16},{17,1},{1,17},{18,2},{2,18},{19,3},{3,19},{20,4},{4,... | collective-permute-start | bytes 147464 | tf_op jit(solution)/shard_map/ppermute | solution.py:246
  124.2 11.4 %collective-permute-start.19 = (f32[3,10,1,128]{3,1,2,0:T(8,128)S(1)}, f32[3,10,1,128]{3,1,2,0:T(8,128)S(1)}, u32[]{:S(2)}, u32[]{:S(2)}) collective-permute-start(f32[3,10,1,128]{3,1,2,0:T(8,128)S(1)} %copy.82), channel_id=1, source_target_pairs={{2,0},{4,2},{6,4},{8,6},{10,8},{12,10},{14,12},{0,14},{3,1},{5,3},... | collective-permute-start | bytes 46088 | tf_op jit(solution)/shard_map/ppermute | solution.py:246
  124.3 8.3 %collective-permute-start.18 = (f32[3,10,1,128]{3,1,2,0:T(8,128)S(1)}, f32[3,10,1,128]{3,1,2,0:T(8,128)S(1)}, u32[]{:S(2)}, u32[]{:S(2)}) collective-permute-start(f32[3,10,1,128]{3,1,2,0:T(8,128)S(1)} %copy.81), channel_id=1, source_target_pairs={{0,2},{2,4},{4,6},{6,8},{8,10},{10,12},{12,14},{14,0},{1,3},{3,5},... | collective-permute-start | bytes 46088 | tf_op jit(solution)/shard_map/ppermute | solution.py:245
  125.4 19.3 %collective-permute-start.22 = (f32[3,1024]{1,0:T(4,128)}, f32[3,1024]{1,0:T(4,128)}, u32[]{:S(2)}, u32[]{:S(2)}) collective-permute-start(f32[3,1024]{1,0:T(4,128)} %get-tuple-element.54), channel_id=1, source_target_pairs={{0,16},{16,0},{1,17},{17,1},{2,18},{18,2},{3,19},{19,3},{4,20},{20... | collective-permute-start | bytes 36872 | tf_op jit(solution)/shard_map/ppermute | solution.py:235
  126.8 19.2 %collective-permute-start.25 = (f32[3,1024]{1,0:T(4,128)}, f32[3,1024]{1,0:T(4,128)}, u32[]{:S(2)}, u32[]{:S(2)}) collective-permute-start(f32[3,1024]{1,0:T(4,128)} %get-tuple-element.55), channel_id=1, source_target_pairs={{0,2},{2,4},{4,6},{6,8},{8,10},{10,12},{12,14},{14,0},{1,3},{3,5},... | collective-permute-start | bytes 36872 | tf_op jit(solution)/shard_map/ppermute | solution.py:235
  126.8 19.2 %collective-permute-start.24 = (f32[3,1024]{1,0:T(4,128)}, f32[3,1024]{1,0:T(4,128)}, u32[]{:S(2)}, u32[]{:S(2)}) collective-permute-start(f32[3,1024]{1,0:T(4,128)} %get-tuple-element.56), channel_id=1, source_target_pairs={{0,14},{2,0},{4,2},{6,4},{8,6},{10,8},{12,10},{14,12},{1,15},{3,1}... | collective-permute-start | bytes 36872 | tf_op jit(solution)/shard_map/ppermute | solution.py:235
  132.6 13.3 %collective-permute-start.23 = (f32[3,1024]{1,0:T(4,128)S(1)}, f32[3,1024]{1,0:T(4,128)}, u32[]{:S(2)}, u32[]{:S(2)}) collective-permute-start(f32[3,1024]{1,0:T(4,128)S(1)} %get-tuple-element.57), channel_id=1, source_target_pairs={{0,16},{16,0},{1,17},{17,1},{2,18},{18,2},{3,19},{19,3},{4,20},{20... | collective-permute-start | bytes 36872 | tf_op jit(solution)/shard_map/ppermute | solution.py:235
  143.9 6.6 %collective-permute-start.20 = (f32[3,10,34,1]{2,1,3,0:T(8,128)}, f32[3,10,34,1]{2,1,3,0:T(8,128)}, u32[]{:S(2)}, u32[]{:S(2)}) collective-permute-start(f32[3,10,34,1]{2,1,3,0:T(8,128)} %get-tuple-element.34), channel_id=1, source_target_pairs={{0,1},{1,0},{2,3},{3,2},{4,5},{5,4},{6,7},{7,6},{8,9},{9,8},{10,11... | collective-permute-start | bytes 12248 | tf_op jit(solution)/shard_map/ppermute | solution.py:245
  144.8 4.6 %collective-permute-start.21 = (f32[3,10,34,1]{2,1,3,0:T(8,128)}, f32[3,10,34,1]{2,1,3,0:T(8,128)}, u32[]{:S(2)}, u32[]{:S(2)}) collective-permute-start(f32[3,10,34,1]{2,1,3,0:T(8,128)} %get-tuple-element.35), channel_id=1, source_target_pairs={{1,0},{0,1},{3,2},{2,3},{5,4},{4,5},{7,6},{6,7},{9,8},{8,9},{11,10... | collective-permute-start | bytes 12248 | tf_op jit(solution)/shard_map/ppermute | solution.py:246
  149.3 3.9 %copy-start.6 = (f32[8,32,128]{2,1,0:T(8,128)S(1)}, f32[8,32,128]{2,1,0:T(8,128)}, u32[]{:S(2)}) copy-start(f32[8,32,128]{2,1,0:T(8,128)} %copy-done.4) | copy-start | bytes 393220
  149.3 3.9 %copy-start.9 = (f32[8,32,128]{2,1,0:T(8,128)S(1)}, f32[8,32,128]{2,1,0:T(8,128)}, u32[]{:S(2)}) copy-start(f32[8,32,128]{2,1,0:T(8,128)} %copy-done.7) | copy-start | bytes 393220
  149.3 3.9 %copy-start.12 = (f32[8,32,128]{2,1,0:T(8,128)S(1)}, f32[8,32,128]{2,1,0:T(8,128)}, u32[]{:S(2)}) copy-start(f32[8,32,128]{2,1,0:T(8,128)} %copy-done.10) | copy-start | bytes 393220
  149.3 3.9 %copy-start.15 = (f32[8,32,128]{2,1,0:T(8,128)S(1)}, f32[8,32,128]{2,1,0:T(8,128)}, u32[]{:S(2)}) copy-start(f32[8,32,128]{2,1,0:T(8,128)} %copy-done.13) | copy-start | bytes 393220
  149.3 3.9 %copy-start.18 = (f32[8,32,128]{2,1,0:T(8,128)S(1)}, f32[8,32,128]{2,1,0:T(8,128)}, u32[]{:S(2)}) copy-start(f32[8,32,128]{2,1,0:T(8,128)} %copy-done.16) | copy-start | bytes 393220
  149.3 3.9 %copy-start.21 = (f32[8,32,128]{2,1,0:T(8,128)S(1)}, f32[8,32,128]{2,1,0:T(8,128)}, u32[]{:S(2)}) copy-start(f32[8,32,128]{2,1,0:T(8,128)} %copy-done.19) | copy-start | bytes 393220
  149.3 3.9 %copy-start.24 = (f32[8,32,128]{2,1,0:T(8,128)S(1)}, f32[8,32,128]{2,1,0:T(8,128)}, u32[]{:S(2)}) copy-start(f32[8,32,128]{2,1,0:T(8,128)} %copy-done.22) | copy-start | bytes 393220

commit v2 on v1

--- a/solution.py
+++ b/solution.py
@@ -229,119 +229,213 @@
     )
 
 
-def passed_along(value, axis, steps):
-    count = lax.axis_size(axis)
-    pairs = [(source, (source + steps) % count) for source in range(count)]
-    return lax.ppermute(value, axis, pairs)
-
-
-def padded(array, sides, width):
-    for axis, dim in sides:
-        devices, length = (lax.axis_size(axis), array.shape[dim])
-        up = [(i, (i + 1) % devices) for i in range(devices)]
-        down = [(j, i) for i, j in up]
-        last = lax.slice_in_dim(array, length - width, length, axis=dim)
-        leading = lax.slice_in_dim(array, 0, width, axis=dim)
-        before = lax.ppermute(last, axis, up)
-        after = lax.ppermute(leading, axis, down)
-        array = jnp.concatenate([before, array, after], axis=dim)
-    return array
-
-
-def fibre_terms(fibre_vel, fluid_vel, fibre_props):
-    volume = fibre_props[0][None, :]
-    drag_force = fibre_props[1][None, :] * (fluid_vel - fibre_vel)
-    moved_vel = fibre_vel + drag_step * drag_force / volume
-    partials = jnp.concatenate([drag_force, volume], axis=0)
-    return (partials, moved_vel)
-
-
-def adjacent_value(grid_field, axis_location, upper_value):
-    leading = grid_field.ndim - 3
-    result = grid_field
-    for position in range(3):
-        length = grid_field.shape[leading + position]
-        start = 1
-        if position == axis_location:
-            start = 2 if upper_value else 0
-        result = lax.slice_in_dim(result, start, start + length - 2, axis=leading + position)
-    return result
-
-
-def relaxation_pass(bordered_velocity, bordered_porosity, momentum_source):
-    central_value = bordered_porosity[1:-1, 1:-1, 1:-1]
-    weight_sum = jnp.zeros_like(central_value)
-    flux_sum = jnp.zeros_like(momentum_source)
-    for axis_location in range(3):
-        for upper_value in (False, True):
-            blend_weight = 0.5 * (
-                central_value + adjacent_value(bordered_porosity, axis_location, upper_value)
-            )
-            weight_sum = weight_sum + blend_weight
-            flux_sum = flux_sum + blend_weight[None] * adjacent_value(
-                bordered_velocity, axis_location, upper_value
-            )
-    return (momentum_source + coupling * flux_sum) / (central_value + coupling * weight_sum)[None]
-
-
-def wall_cells(brick_depth, margin):
-    heights = (
-        lax.axis_index("gz") * brick_depth
-        + jnp.arange(brick_depth + 2 * margin, dtype=jnp.int32)
-        - margin
-    )
-    return (heights < 0) | (heights >= brick_depth * lax.axis_size("gz"))
+MESH = pl.DeviceIdType.MESH
+
+
+def sweep_kernel(
+    velocity, dep, rows, mov,
+    out, arrivals,
+    got_rows, got_mov, u1, u2, phi, src, wts, inv, sy, sz, hx, hy, hz,
+    row_send, row_recv, mov_send, mov_recv, face_send, face_recv,
+):
+    wide_x, wide_y = velocity.shape[1], velocity.shape[2]
+    slots = rows.shape[1] - 8
+    near = []
+    for axis in ("gx", "gy", "gz"):
+        n = lax.axis_size(axis)
+        me = lax.axis_index(axis)
+        near.append({axis: lax.rem(me + n - 1, n)})
+        near.append({axis: lax.rem(me + 1, n)})
+
+    barrier = pltpu.get_barrier_semaphore()
+    for device in near:
+        pl.semaphore_signal(barrier, inc=1, device_id=device, device_id_type=MESH)
+    pl.semaphore_wait(barrier, 6)
+
+    copies = []
+
+    def send(source, target, send_sem, recv_sem, device):
+        copy = pltpu.make_async_remote_copy(
+            src_ref=source, dst_ref=target, send_sem=send_sem, recv_sem=recv_sem,
+            device_id=device, device_id_type=MESH,
+        )
+        copy.start()
+        copies.append(copy)
+        return copy
+
+    row_copies = [
+        send(rows.at[d], got_rows.at[d], row_send.at[d], row_recv.at[d], near[d]) for d in range(4)
+    ]
+
+    sub = lax.broadcasted_iota(jnp.int32, (wide_y, LANES), 0)
+    lane = lax.broadcasted_iota(jnp.int32, (wide_y, LANES), 1)
+
+    def send_faces(phase, field, count):
+        total = count * wide_x
+        started = []
+        started.append(send(
+            field.at[:, 0], hx.at[phase, 1, pl.ds(0, count)],
+            face_send.at[phase, 0], face_recv.at[phase, 1], near[0],
+        ))
+        started.append(send(
+            field.at[:, wide_x - 1], hx.at[phase, 0, pl.ds(0, count)],
+            face_send.at[phase, 1], face_recv.at[phase, 0], near[1],
+        ))
+        low = jnp.zeros((wide_y, LANES), F32)
+        high = jnp.zeros((wide_y, LANES), F32)
+        for j in range(total):
+            plane = field[j // wide_x, j % wide_x]
+            sy[phase, 0, j:j + 1, :] = plane[0:1, :]
+            sy[phase, 1, j:j + 1, :] = plane[wide_y - 1:wide_y, :]
+            low = jnp.where(lane == j, pltpu.roll(plane, j, 1) if j else plane, low)
+            high = jnp.where(lane == j, pltpu.roll(plane, j + 1, 1), high)
+        for side in range(2):
+            started.append(send(
+                sy.at[phase, side, pl.ds(0, total)], hy.at[phase, 1 - side, pl.ds(0, total)],
+                face_send.at[phase, 2 + side], face_recv.at[phase, 3 - side], near[2 + side],
+            ))
+        sz[phase, 0] = low
+        sz[phase, 1] = high
+        for side in range(2):
+            started.append(send(
+                sz.at[phase, side], hz.at[phase, 1 - side],
+                face_send.at[phase, 4 + side], face_recv.at[phase, 5 - side], near[4 + side],
+            ))
+        return started
+
+    def arrive(started):
+        for copy in started:
+            copy.wait_recv()
+
+    bottom = lax.axis_index("gz") == 0
+    top = lax.axis_index("gz") == lax.axis_size("gz") - 1
+
+    def z_halos(phase, wall):
+        return (
+            jnp.where(bottom, wall, hz[phase, 0]),
+            jnp.where(top, wall, hz[phase, 1]),
+        )
+
+    def around(phase, field, c, x, z_low, z_high):
+        j = c * wide_x + x
+        here = field[c, x]
+        x_low = field[c, x - 1] if x > 0 else hx[phase, 0, c]
+        x_high = field[c, x + 1] if x < wide_x - 1 else hx[phase, 1, c]
+        y_low = jnp.where(sub == 0, hy[phase, 0, j:j + 1, :], pltpu.roll(here, 1, 0))
+        y_high = jnp.where(
+            sub == wide_y - 1, hy[phase, 1, j:j + 1, :], pltpu.roll(here, wide_y - 1, 0)
+        )
+        edge_low = pltpu.roll(z_low, LANES - j, 1) if j else z_low
+        edge_high = pltpu.roll(z_high, LANES - 1 - j, 1)
+        below = jnp.where(lane == 0, edge_low, pltpu.roll(here, 1, 1))
+        above = jnp.where(lane == LANES - 1, edge_high, pltpu.roll(here, LANES - 1, 1))
+        return here, (x_low, x_high, y_low, y_high, below, above)
+
+    first = send_faces(0, velocity, 3)
+    mov_copies = [
+        send(mov.at[d], got_mov.at[d], mov_send.at[d], mov_recv.at[d], near[d]) for d in range(4)
+    ]
+
+    extra = jnp.zeros((wide_x * wide_y, 4 * LANES), F32)
+    row_no = lax.broadcasted_iota(jnp.int32, (wide_x * wide_y, slots), 0).astype(F32)
+    for d in range(4):
+        row_copies[d].wait_recv()
+        ids = got_rows[d, slots:slots + 1, 0:slots]
+        hot = jnp.where(row_no == ids, 1.0, 0.0).astype(BF16)
+        hi, lo = parts_of(got_rows[d, 0:slots, :])
+        extra = extra + jnp.dot(hot, hi, preferred_element_type=F32)
+        extra = extra + jnp.dot(hot, lo, preferred_element_type=F32)
+    fraction = 1.0 / (1.0 + (dep[3] + extra[:, 3 * LANES:]))
+    phi[...] = fraction.reshape(1, wide_x, wide_y, LANES)
+    second = send_faces(1, phi, 1)
+    for c in range(3):
+        drag = (dep[c] + extra[:, c * LANES:(c + 1) * LANES]).reshape(wide_x, wide_y, LANES)
+        src[c] = phi[0] * velocity[c] - source_step * drag
+
+    arrive(second)
+    z_low, z_high = z_halos(1, 1.0)
+    for x in range(wide_x):
+        here, others = around(1, phi, 0, x, z_low, z_high)
+        total = jnp.zeros_like(here)
+        for k in range(6):
+            weight = 0.5 * (here + others[k])
+            wts[k, x] = weight
+            total = total + weight
+        inv[x] = 1.0 / (here + coupling * total)
+
+    def sweep(phase, field, target):
+        z_low, z_high = z_halos(phase, 0.0)
+        for x in range(wide_x):
+            for c in range(3):
+                here, others = around(phase, field, c, x, z_low, z_high)
+                flux = wts[0, x] * others[0]
+                for k in range(1, 6):
+                    flux = flux + wts[k, x] * others[k]
+                target[c, x] = (src[c, x] + coupling * flux) * inv[x]
+
+    arrive(first)
+    sweep(0, velocity, u1)
+    third = send_faces(2, u1, 3)
+    for d in range(4):
+        mov_copies[d].wait_recv()
+        arrivals[d] = got_mov[d]
+    arrive(third)
+    sweep(2, u1, u2)
+    fourth = send_faces(3, u2, 3)
+    arrive(fourth)
+    sweep(3, u2, out)
+    for copy in copies:
+        copy.wait_send()
+
+
+def sweeps(velocity, deposit, rows, movers):
+    _, wide_x, wide_y, wide_z = velocity.shape
+    vm = pl.BlockSpec(memory_space=pltpu.VMEM)
+    sem = pltpu.SemaphoreType.DMA
+    field = (3, wide_x, wide_y, wide_z)
+    return pl.pallas_call(
+        sweep_kernel,
+        out_shape=(
+            jax.ShapeDtypeStruct(velocity.shape, F32),
+            jax.ShapeDtypeStruct(movers.shape, F32),
+        ),
+        in_specs=[vm] * 4,
+        out_specs=(vm,) * 2,
+        scratch_shapes=[
+            pltpu.VMEM(rows.shape, F32),
+            pltpu.VMEM(movers.shape, F32),
+            pltpu.VMEM(field, F32),
+            pltpu.VMEM(field, F32),
+            pltpu.VMEM((1,) + field[1:], F32),
+            pltpu.VMEM(field, F32),
+            pltpu.VMEM((6,) + field[1:], F32),
+            pltpu.VMEM(field[1:], F32),
+            pltpu.VMEM((4, 2, 3 * wide_x, wide_z), F32),
+            pltpu.VMEM((4, 2, wide_y, wide_z), F32),
+            pltpu.VMEM((4, 2, 3, wide_y, wide_z), F32),
+            pltpu.VMEM((4, 2, 3 * wide_x, wide_z), F32),
+            pltpu.VMEM((4, 2, wide_y, wide_z), F32),
+            sem((4,)), sem((4,)), sem((4,)), sem((4,)), sem((4, 6)), sem((4, 6)),
+        ],
+        compiler_params=pltpu.CompilerParams(
+            collective_id=0, has_side_effects=True, vmem_limit_bytes=32 * 1024 * 1024
+        ),
+        cost_estimate=pl.CostEstimate(flops=20_000_000, bytes_accessed=2_000_000, transcendentals=0),
+        name="sweeps",
+    )(velocity, deposit, rows, movers)
 
 
 def body(
-    velocity,
-    fibre_vel,
-    fluid_vel,
-    fibre_props,
-    fibre_row,
-    fibre_height,
-    migrant_list,
-    migrant_slot,
-    side_rows,
+    velocity, fibre_vel, fluid_vel, fibre_props, fibre_row, fibre_height,
+    migrant_list, migrant_slot, side_rows,
 ):
-    width_x, width_y, width_z = (velocity.shape[1], velocity.shape[2], velocity.shape[3])
-    row_count = width_x * width_y
-    cell_count = row_count * width_z
-    slot_count = side_rows.shape[1]
+    row_count = velocity.shape[1] * velocity.shape[2]
     kept_fibres, deposit, rows, movers = local_part(
         fibre_vel, fluid_vel, fibre_props, fibre_row, fibre_height,
         migrant_list, migrant_slot, side_rows, row_count,
     )
-    arrived = []
-    for direction in range(4):
-        step_by = 1 if direction % 2 == 1 else -1
-        got_rows, got_vel = passed_along(
-            (rows[direction], movers[direction]), "gx" if direction < 2 else "gy", step_by
-        )
-        got_ids = got_rows[slot_count, :slot_count].astype(jnp.int32)
-        moved_rows = got_rows[:slot_count].reshape(slot_count, 4, width_z).transpose(1, 0, 2)
-        deposit = deposit.at[:, got_ids].add(moved_rows)
-        arrived.append(got_vel)
-    drag_field = deposit[0:3].reshape(3, width_x, width_y, width_z)
-    void_fraction = 1.0 / (1.0 + deposit[3].reshape(width_x, width_y, width_z))
-    momentum_source = void_fraction[None] * velocity - source_step * drag_field
-    boundary_mask = wall_cells(width_z, 1)
-    bordered_field = padded(
-        jnp.concatenate([velocity, void_fraction[None]], axis=0),
-        (("gx", 1), ("gy", 2), ("gz", 3)),
-        1,
-    )
-    bordered_porosity = jnp.where(boundary_mask, 1.0, bordered_field[3])
-    present_velocity = relaxation_pass(
-        jnp.where(boundary_mask, 0.0, bordered_field[0:3]), bordered_porosity, momentum_source
-    )
-    for sweep_index in range(SWEEPS - 1):
-        bordered_velocity = padded(present_velocity, (("gx", 1), ("gy", 2), ("gz", 3)), 1)
-        present_velocity = relaxation_pass(
-            jnp.where(boundary_mask, 0.0, bordered_velocity), bordered_porosity, momentum_source
-        )
-    arrivals = jnp.stack(arrived, axis=0)
-    return (present_velocity, kept_fibres, arrivals)
+    new_velocity, arrivals = sweeps(velocity, deposit, rows, movers)
+    return new_velocity, kept_fibres, arrivals
 
 
 def solution(mesh):

time: 155 us -> 65 us (0.42)
  local copies, waits for them, and re-layouts: 41.6 us -> 4.21 us
  starting transfers between devices: 32.3 us -> 0 us
  other arithmetic: 30.1 us -> 0 us
  Pallas kernels: 36.9 us -> 59.8 us
  waiting for transfers between devices: 12.4 us -> 0 us
    ppermute x26 -> x0, starting transfers between devices: 32.3 us -> none  [the longest x9 13.2 us: padded(): after = lax.ppermute(leading, axis, down)]
    pallas_call x0 -> x1, Pallas kernels: none -> 22.9 us  [sweeps(): pl.pallas_call(sweep_kernel, out_shape=(jax.ShapeDtypeStruct(velocity.sha...]
    ppermute x12 -> x0, local copies, waits for them, and re-layouts: 20.2 us -> none  [the longest x6 10.2 us: padded(): after = lax.ppermute(leading, axis, down)]
    concatenate x6 -> x0, other arithmetic: 17.9 us -> none  [padded(): array = jnp.concatenate([before, array, after], axis=dim)]
    concatenate x6 -> x0, local copies, waits for them, and re-layouts: 14.2 us -> none  [padded(): array = jnp.concatenate([before, array, after], axis=dim)]
    ppermute x26 -> x0, waiting for transfers between devices: 12.4 us -> none  [the longest x9 6.38 us: padded(): before = lax.ppermute(last, axis, up)]
    scatter-add x4 -> x0, other arithmetic: 4.36 us -> none  [body(): deposit = deposit.at[:, got_ids].add(moved_rows)]
    select_n x8 -> x0, other arithmetic: 4.04 us -> none  [the longest x2 3.25 us: body(): jnp.where(boundary_mask, 0.0, bordered_velocity)]
  transfers between devices with their start and end apart: 26 -> 0, of which waited for: 10 -> 0; matrix products, arithmetic and copies ran while one was open for 23% -> 0% of each run, Pallas kernels for 0% -> 0%
where the time goes in v2:
time: 65 us; the launch traced here: 64.7 us
  Pallas kernels  59.8 us (92%)
  local copies, waits for them, and re-layouts  4.21 us (6%)
  between operations  0.66 us (1%)
    pallas_call x1, Pallas kernels, local_part(): pl.pallas_call(local_kernel, out_shape=(jax.ShapeDtypeStruct((3, fibres),...  36.9 us
    pallas_call x1, Pallas kernels, sweeps(): pl.pallas_call(sweep_kernel, out_shape=(jax.ShapeDtypeStruct(velocity.sha...  22.9 us
    unnamed x10, local copies, waits for them, and re-layouts  4.21 us

profile of v2, /device:TPU:0, one launch (start us, length us, event | category | flops | bytes accessed | tf_op | source)
XLA Modules:
  0.0 64.7 jit_solution(14424095888324700902)
XLA Ops:
  0.6 0.0 copy-start.1
  0.6 36.9 %fibres.1 = (f32[3,32768]{1,0:T(4,128)}, f32[4,256,128]{2,1,0:T(8,128)}, f32[4,24,512]{2,1,0:T(8,128)}, f32[4,3,1024]{2,1,0:T(4,128)}) custom-call(f32[3,32768]{1,0:T(4,128)} %vel.1, f32[3,32768]{1,0:T(4,128)} %flu.1, f32[2,32768]{1,0:T(2,128)} %prop.1, s32[256,128]{1,0:T(8,128)} %bitcast.2, s32[256,128]{1,0:T(8,128)} %bitcast.3, s32[4,1024]{1,0:T(4,128)} %mlist.1, ...), custom_call_target="tpu_custom_call" | custom-call | flops 16999999488 | bytes 3000000 | tf_op jit(solution)/shard_map/fibres/pallas_call | solution.py:197
  37.6 0.0 copy-done.1
  37.6 0.0 copy-start
  37.6 1.0 %copy-done = f32[4,256,128]{2,1,0:T(8,128)S(1)} copy-done((f32[4,256,128]{2,1,0:T(8,128)S(1)}, f32[4,256,128]{2,1,0:T(8,128)}, u32[]{:S(2)}) %copy-start) | copy-done | bytes 524312
  38.6 0.0 copy-start.2
  38.6 0.9 %copy-done.2 = f32[4,24,512]{2,1,0:T(8,128)S(1)} copy-done((f32[4,24,512]{2,1,0:T(8,128)S(1)}, f32[4,24,512]{2,1,0:T(8,128)}, u32[]{:S(2)}) %copy-start.2) | copy-done | bytes 196632
  39.5 0.0 copy-start.3
  39.5 0.8 %copy-done.3 = f32[4,3,1024]{2,1,0:T(4,128)S(1)} copy-done((f32[4,3,1024]{2,1,0:T(4,128)S(1)}, f32[4,3,1024]{2,1,0:T(4,128)}, u32[]{:S(2)}) %copy-start.3) | copy-done | bytes 49176
  40.4 22.9 %sweeps.1 = (f32[3,8,32,128]{3,2,1,0:T(8,128)S(1)}, f32[4,3,1024]{2,1,0:T(4,128)S(1)}) custom-call(f32[3,8,32,128]{3,2,1,0:T(8,128)S(1)} %copy-done.1, f32[4,256,128]{2,1,0:T(8,128)S(1)} %copy-done, f32[4,24,512]{2,1,0:T(8,128)S(1)} %copy-done.2, f32[4,3,1024]{2,1,0:T(4,128)S(1)} %copy-done.3), custom_call_target="tpu_custom_call" | custom-call | flops 20000000 | bytes 2000000 | tf_op jit(solution)/shard_map/sweeps/pallas_call | solution.py:396
  63.3 0.7 %copy.12 = f32[4,3,1024]{2,0,1:T(4,128)} copy(f32[4,3,1024]{2,1,0:T(4,128)S(1)} %get-tuple-element.17) | data formatting | bytes 98304
  63.9 0.7 %copy.14 = f32[3,8,32,128]{3,2,1,0:T(8,128)} copy(f32[3,8,32,128]{3,2,1,0:T(8,128)S(1)} %get-tuple-element.21) | data formatting | bytes 786432
Async XLA Ops:
  0.6 36.9 %copy-start.1 = (f32[3,8,32,128]{3,2,1,0:T(8,128)S(1)}, f32[3,8,32,128]{3,2,1,0:T(8,128)}, u32[]{:S(2)}) copy-start(f32[3,8,32,128]{3,2,1,0:T(8,128)} %velocity.1) | copy-start | bytes 1179652
  37.6 1.0 %copy-start = (f32[4,256,128]{2,1,0:T(8,128)S(1)}, f32[4,256,128]{2,1,0:T(8,128)}, u32[]{:S(2)}) copy-start(f32[4,256,128]{2,1,0:T(8,128)} %get-tuple-element.9.dep) | copy-start | bytes 1572868
  38.6 0.9 %copy-start.2 = (f32[4,24,512]{2,1,0:T(8,128)S(1)}, f32[4,24,512]{2,1,0:T(8,128)}, u32[]{:S(2)}) copy-start(f32[4,24,512]{2,1,0:T(8,128)} %get-tuple-element.10.rows) | copy-start | bytes 589828
  39.5 0.8 %copy-start.3 = (f32[4,3,1024]{2,1,0:T(4,128)S(1)}, f32[4,3,1024]{2,1,0:T(4,128)}, u32[]{:S(2)}) copy-start(f32[4,3,1024]{2,1,0:T(4,128)} %get-tuple-element.11.mov) | copy-start | bytes 147460

commit v3 on v2

--- a/solution.py
+++ b/solution.py
@@ -35,13 +35,30 @@
     return jnp.concatenate(out, axis=0)
 
 
-def local_kernel(
-    vel, flu, prop, row, height, mlist, mslot, side,
-    kept, dep, rows, mov,
-    st_vel, st_flu, st_prop, tabs, moved_t, gt_hi, gt_lo, gath, b0, a0, b1, a1, acc,
+MESH = pl.DeviceIdType.MESH
+
+
+def step_kernel(
+    velocity, vel, flu, prop, row, height, mlist, mslot, side,
+    out, kept, arrivals,
+    st_vel, st_flu, st_prop, tabs, gt_hi, gt_lo, gath, b0, a0, b1, a1, acc, dep, rows, mov,
+    got_rows, got_mov, u1, u2, phi, src, wts, inv, sy, sz, hx, hy, hz,
+    row_send, row_recv, mov_send, mov_recv, face_send, face_recv,
 ):
+    wide_x, wide_y = velocity.shape[1], velocity.shape[2]
+    near = []
+    for axis in ("gx", "gy", "gz"):
+        n = lax.axis_size(axis)
+        me = lax.axis_index(axis)
+        near.append({axis: lax.rem(me + n - 1, n)})
+        near.append({axis: lax.rem(me + 1, n)})
+
+    barrier = pltpu.get_barrier_semaphore()
+    for device in near:
+        pl.semaphore_signal(barrier, inc=1, device_id=device, device_id_type=MESH)
+
     groups = row.shape[0]
-    row_count = dep.shape[1]
+    row_count = wide_x * wide_y
     migs = mlist.shape[1]
     slots = side.shape[1]
 
@@ -81,7 +98,6 @@
         hi, lo = parts_of(force)
         tabs[c] = hi.astype(F32)
         tabs[4 + c] = lo.astype(F32)
-        moved_t[c] = moved
         hi, lo = parts_of(force.T)
         gt_hi[c * LANES:(c + 1) * LANES, :] = hi
         gt_lo[c * LANES:(c + 1) * LANES, :] = lo
@@ -146,110 +162,11 @@
         slot_hot = one_hot(spread16(mslot[d:d + 1, :].astype(F32)), slots, iota16)
         block_rows = lax.dot_general(slot_hot, b0[:, :migs], NT, preferred_element_type=F32)
         rows[d, 0:slots, :] = block_rows[:, :4 * LANES] + block_rows[:, 4 * LANES:]
-        rows[d, slots:slots + 1, 0:slots] = side[d:d + 1, :].astype(F32)
-
-    iota_l = iota16[:, :LANES]
-
-    def build(group0, b, a):
-        for k in range(GROUP):
-            g = group0 + k
-            cols = slice(k * LANES, (k + 1) * LANES)
-            h16 = spread16(tabs[8, pl.ds(g, 1), :])
-            r16 = spread16(tabs[9, pl.ds(g, 1), :])
-            hits = [iota_l == h16 - float(16 * block) for block in range(LANES // 16)]
-            for p in range(8):
-                v16 = spread16(tabs[p, pl.ds(g, 1), :])
-                for block in range(LANES // 16):
-                    base = p * LANES + block * 16
-                    b[base:base + 16, cols] = jnp.where(hits[block], v16, jnp.zeros((), BF16))
-            for block in range(row_count // 16):
-                a[block * 16:(block + 1) * 16, cols] = jnp.where(
-                    iota_l == r16 - float(16 * block), jnp.ones((), BF16), jnp.zeros((), BF16)
-                )
-
-    def add(b, a):
-        acc[...] += lax.dot_general(b[...], a[...], NT, preferred_element_type=F32)
-
-    acc[...] = jnp.zeros_like(acc)
-    build(0, b0, a0)
-    pairs = groups // (2 * GROUP)
-
-    def deposit(step, carry):
-        build(step * 2 * GROUP + GROUP, b1, a1)
-        add(b0, a0)
-        build(jnp.minimum(step + 1, pairs - 1) * 2 * GROUP, b0, a0)
-        add(b1, a1)
-        return carry
-
-    lax.fori_loop(0, pairs, deposit, 0)
-    for f in range(4):
-        total = acc[f * LANES:(f + 1) * LANES, :] + acc[(4 + f) * LANES:(5 + f) * LANES, :]
-        dep[f] = total.T
-
-
-def local_part(fibre_vel, fluid_vel, fibre_props, fibre_row, fibre_height, migrant_list, migrant_slot, side_rows, row_count):
-    fibres = fibre_vel.shape[1]
-    groups = fibres // LANES
-    migs = migrant_list.shape[1]
-    slots = side_rows.shape[1]
-    wide = GROUP * LANES
-    vm = pl.BlockSpec(memory_space=pltpu.VMEM)
-    return pl.pallas_call(
-        local_kernel,
-        out_shape=(
-            jax.ShapeDtypeStruct((3, fibres), F32),
-            jax.ShapeDtypeStruct((4, row_count, LANES), F32),
-            jax.ShapeDtypeStruct((4, slots + 8, 4 * LANES), F32),
-            jax.ShapeDtypeStruct((4, 3, migs), F32),
-        ),
-        in_specs=[vm] * 8,
-        out_specs=(vm,) * 4,
-        scratch_shapes=[
-            pltpu.VMEM((groups * 8, LANES), F32),
-            pltpu.VMEM((groups * 8, LANES), F32),
-            pltpu.VMEM((groups * 8, LANES), F32),
-            pltpu.VMEM((10, groups, LANES), F32),
-            pltpu.VMEM((3, groups, LANES), F32),
-            pltpu.VMEM((8 * LANES, groups), BF16),
-            pltpu.VMEM((7 * LANES, groups), BF16),
-            pltpu.VMEM((8, migs), F32),
-            pltpu.VMEM((8 * LANES, wide), BF16),
-            pltpu.VMEM((row_count, wide), BF16),
-            pltpu.VMEM((8 * LANES, wide), BF16),
-            pltpu.VMEM((row_count, wide), BF16),
-            pltpu.VMEM((8 * LANES, row_count), F32),
-        ],
-        compiler_params=pltpu.CompilerParams(vmem_limit_bytes=56 * 1024 * 1024),
-        cost_estimate=pl.CostEstimate(flops=17_000_000_000, bytes_accessed=3_000_000, transcendentals=0),
-        name="fibres",
-    )(
-        fibre_vel, fluid_vel, fibre_props,
-        fibre_row.reshape(groups, LANES), fibre_height.reshape(groups, LANES),
-        migrant_list, migrant_slot, side_rows,
-    )
-
-
-MESH = pl.DeviceIdType.MESH
-
-
-def sweep_kernel(
-    velocity, dep, rows, mov,
-    out, arrivals,
-    got_rows, got_mov, u1, u2, phi, src, wts, inv, sy, sz, hx, hy, hz,
-    row_send, row_recv, mov_send, mov_recv, face_send, face_recv,
-):
-    wide_x, wide_y = velocity.shape[1], velocity.shape[2]
-    slots = rows.shape[1] - 8
-    near = []
-    for axis in ("gx", "gy", "gz"):
-        n = lax.axis_size(axis)
-        me = lax.axis_index(axis)
-        near.append({axis: lax.rem(me + n - 1, n)})
-        near.append({axis: lax.rem(me + 1, n)})
-
-    barrier = pltpu.get_barrier_semaphore()
-    for device in near:
-        pl.semaphore_signal(barrier, inc=1, device_id=device, device_id_type=MESH)
+        ids = side[d:d + 1, :].astype(F32)
+        rows[d, slots:slots + 8, :] = jnp.zeros((8, 4 * LANES), F32)
+        rows[d, slots:slots + 1, d * slots:(d + 1) * slots] = ids
+        rows[d, slots:slots + 1, (4 + d) * slots:(5 + d) * slots] = ids
+
     pl.semaphore_wait(barrier, 6)
 
     copies = []
@@ -336,15 +253,50 @@
         send(mov.at[d], got_mov.at[d], mov_send.at[d], mov_recv.at[d], near[d]) for d in range(4)
     ]
 
-    extra = jnp.zeros((wide_x * wide_y, 4 * LANES), F32)
-    row_no = lax.broadcasted_iota(jnp.int32, (wide_x * wide_y, slots), 0).astype(F32)
+    cell_no = iota16[:, :LANES]
+    height_no = jnp.stack([cell_no + float(16 * k) for k in range(LANES // 16)], axis=0)
+    group_row_no = jnp.stack([cell_no + float(16 * k) for k in range(row_count // 16)], axis=0)
+    nought, one = jnp.zeros((), BF16), jnp.ones((), BF16)
+
+    def build(group0, b, a):
+        for k in range(GROUP):
+            g = group0 + k
+            cols = slice(k * LANES, (k + 1) * LANES)
+            hits = height_no == spread16(tabs[8, pl.ds(g, 1), :])[None]
+            for p in range(8):
+                v16 = spread16(tabs[p, pl.ds(g, 1), :])
+                b[p * LANES:(p + 1) * LANES, cols] = jnp.where(hits, v16[None], nought).reshape(LANES, LANES)
+            hits = group_row_no == spread16(tabs[9, pl.ds(g, 1), :])[None]
+            a[:, cols] = jnp.where(hits, one, nought).reshape(row_count, LANES)
+
+    def add(b, a):
+        acc[...] += lax.dot_general(b[...], a[...], NT, preferred_element_type=F32)
+
+    acc[...] = jnp.zeros_like(acc)
+    build(0, b0, a0)
+    pairs = groups // (2 * GROUP)
+
+    def deposit(step, carry):
+        build(step * 2 * GROUP + GROUP, b1, a1)
+        add(b0, a0)
+        build(jnp.minimum(step + 1, pairs - 1) * 2 * GROUP, b0, a0)
+        add(b1, a1)
+        return carry
+
+    lax.fori_loop(0, pairs, deposit, 0)
+    for f in range(4):
+        total = acc[f * LANES:(f + 1) * LANES, :] + acc[(4 + f) * LANES:(5 + f) * LANES, :]
+        dep[f] = total.T
+
+
     for d in range(4):
         row_copies[d].wait_recv()
-        ids = got_rows[d, slots:slots + 1, 0:slots]
-        hot = jnp.where(row_no == ids, 1.0, 0.0).astype(BF16)
-        hi, lo = parts_of(got_rows[d, 0:slots, :])
-        extra = extra + jnp.dot(hot, hi, preferred_element_type=F32)
-        extra = extra + jnp.dot(hot, lo, preferred_element_type=F32)
+    row_no = lax.broadcasted_iota(jnp.int32, (row_count, 8 * slots), 0).astype(F32)
+    ids = sum(got_rows[d, slots:slots + 1, 0:8 * slots] for d in range(4))
+    hot = jnp.where(row_no == ids, 1.0, 0.0).astype(BF16)
+    pieces = [parts_of(got_rows[d, 0:slots, :]) for d in range(4)]
+    depth = jnp.concatenate([p[0] for p in pieces] + [p[1] for p in pieces], axis=0)
+    extra = jnp.dot(hot, depth, preferred_element_type=F32)
     fraction = 1.0 / (1.0 + (dep[3] + extra[:, 3 * LANES:]))
     phi[...] = fraction.reshape(1, wide_x, wide_y, LANES)
     second = send_faces(1, phi, 1)
@@ -388,22 +340,48 @@
         copy.wait_send()
 
 
-def sweeps(velocity, deposit, rows, movers):
+def whole_step(
+    velocity, fibre_vel, fluid_vel, fibre_props, fibre_row, fibre_height,
+    migrant_list, migrant_slot, side_rows,
+):
     _, wide_x, wide_y, wide_z = velocity.shape
+    row_count = wide_x * wide_y
+    fibres = fibre_vel.shape[1]
+    groups = fibres // LANES
+    migs = migrant_list.shape[1]
+    slots = side_rows.shape[1]
+    wide = GROUP * LANES
     vm = pl.BlockSpec(memory_space=pltpu.VMEM)
     sem = pltpu.SemaphoreType.DMA
     field = (3, wide_x, wide_y, wide_z)
+    rows = (4, slots + 8, 4 * LANES)
     return pl.pallas_call(
-        sweep_kernel,
+        step_kernel,
         out_shape=(
             jax.ShapeDtypeStruct(velocity.shape, F32),
-            jax.ShapeDtypeStruct(movers.shape, F32),
+            jax.ShapeDtypeStruct((3, fibres), F32),
+            jax.ShapeDtypeStruct((4, 3, migs), F32),
         ),
-        in_specs=[vm] * 4,
-        out_specs=(vm,) * 2,
+        in_specs=[vm] * 9,
+        out_specs=(vm,) * 3,
         scratch_shapes=[
-            pltpu.VMEM(rows.shape, F32),
-            pltpu.VMEM(movers.shape, F32),
+            pltpu.VMEM((groups * 8, LANES), F32),
+            pltpu.VMEM((groups * 8, LANES), F32),
+            pltpu.VMEM((groups * 8, LANES), F32),
+            pltpu.VMEM((10, groups, LANES), F32),
+            pltpu.VMEM((8 * LANES, groups), BF16),
+            pltpu.VMEM((7 * LANES, groups), BF16),
+            pltpu.VMEM((8, migs), F32),
+            pltpu.VMEM((8 * LANES, wide), BF16),
+            pltpu.VMEM((row_count, wide), BF16),
+            pltpu.VMEM((8 * LANES, wide), BF16),
+            pltpu.VMEM((row_count, wide), BF16),
+            pltpu.VMEM((8 * LANES, row_count), F32),
+            pltpu.VMEM((4, row_count, LANES), F32),
+            pltpu.VMEM(rows, F32),
+            pltpu.VMEM((4, 3, migs), F32),
+            pltpu.VMEM(rows, F32),
+            pltpu.VMEM((4, 3, migs), F32),
             pltpu.VMEM(field, F32),
             pltpu.VMEM(field, F32),
             pltpu.VMEM((1,) + field[1:], F32),
@@ -418,24 +396,19 @@
             sem((4,)), sem((4,)), sem((4,)), sem((4,)), sem((4, 6)), sem((4, 6)),
         ],
         compiler_params=pltpu.CompilerParams(
-            collective_id=0, has_side_effects=True, vmem_limit_bytes=32 * 1024 * 1024
+            collective_id=0, has_side_effects=True, vmem_limit_bytes=56 * 1024 * 1024
         ),
-        cost_estimate=pl.CostEstimate(flops=20_000_000, bytes_accessed=2_000_000, transcendentals=0),
-        name="sweeps",
-    )(velocity, deposit, rows, movers)
-
-
-def body(
-    velocity, fibre_vel, fluid_vel, fibre_props, fibre_row, fibre_height,
-    migrant_list, migrant_slot, side_rows,
-):
-    row_count = velocity.shape[1] * velocity.shape[2]
-    kept_fibres, deposit, rows, movers = local_part(
-        fibre_vel, fluid_vel, fibre_props, fibre_row, fibre_height,
-        migrant_list, migrant_slot, side_rows, row_count,
+        cost_estimate=pl.CostEstimate(flops=24_000_000_000, bytes_accessed=3_000_000, transcendentals=0),
+        name="step",
+    )(
+        velocity, fibre_vel, fluid_vel, fibre_props,
+        fibre_row.reshape(groups, LANES), fibre_height.reshape(groups, LANES),
+        migrant_list, migrant_slot, side_rows,
     )
-    new_velocity, arrivals = sweeps(velocity, deposit, rows, movers)
-    return new_velocity, kept_fibres, arrivals
+
+
+def body(*args):
+    return whole_step(*args)
 
 
 def solution(mesh):

time: 65 us -> 59 us (0.908)
  Pallas kernels: 59.8 us -> 54 us
    pallas_call x2 -> x1, Pallas kernels: 59.8 us -> 54 us  [whole_step(): pl.pallas_call(step_kernel, out_shape=(jax.ShapeDtypeStruct(velocity.shap...]
    unnamed x10 -> x4, local copies, waits for them, and re-layouts: 4.21 us -> 2.56 us
    pallas_call x0 -> x1, local copies, waits for them, and re-layouts: none -> 1.55 us  [whole_step(): pl.pallas_call(step_kernel, out_shape=(jax.ShapeDtypeStruct(velocity.shap...]
where the time goes in v3:
time: 59 us; the launch traced here: 58.8 us
  Pallas kernels  54 us (92%)
  local copies, waits for them, and re-layouts  4.11 us (7%)
  between operations  0.65 us (1%)
    pallas_call x1, Pallas kernels, whole_step(): pl.pallas_call(step_kernel, out_shape=(jax.ShapeDtypeStruct(velocity.shap...  54 us
    unnamed x4, local copies, waits for them, and re-layouts  2.56 us
    pallas_call x1, local copies, waits for them, and re-layouts, whole_step(): pl.pallas_call(step_kernel, out_shape=(jax.ShapeDtypeStruct(velocity.shap...  1.55 us

profile of v3, /device:TPU:0, one launch (start us, length us, event | category | flops | bytes accessed | tf_op | source)
XLA Modules:
  0.0 58.8 jit_solution(7736138280947672696)
XLA Ops:
  0.6 54.0 %step.1 = (f32[3,8,32,128]{3,2,1,0:T(8,128)}, f32[3,32768]{1,0:T(4,128)}, f32[4,3,1024]{2,1,0:T(4,128)}) custom-call(f32[3,8,32,128]{3,2,1,0:T(8,128)} %velocity.1, f32[3,32768]{1,0:T(4,128)} %vel.1, f32[3,32768]{1,0:T(4,128)} %flu.1, f32[2,32768]{1,0:T(2,128)} %prop.1, s32[256,128]{1,0:T(8,128)} %bitcast.2, s32[256,128]{1,0:T(8,128)} %bitcast.3, ...), custom_call_target="tpu_custom_call" | custom-call | flops 24000000000 | bytes 3000000 | tf_op jit(solution)/shard_map/step/pallas_call | solution.py:358
  54.6 0.0 copy-start
  54.6 1.6 %copy.12 = f32[4,3,1024]{2,0,1:T(4,128)} copy(f32[4,3,1024]{2,1,0:T(4,128)} %get-tuple-element.5) | data formatting | bytes 98304 | tf_op jit(solution)/shard_map/step/pallas_call | solution.py:358
  56.2 1.8 %copy.15 = f32[3,8,32,128]{3,2,1,0:T(8,128)} copy(f32[3,8,32,128]{3,2,1,0:T(8,128)} %get-tuple-element.9) | data formatting | bytes 786432
  58.0 0.0 copy-done
  58.0 0.8 %copy.16 = f32[3,32768]{1,0:T(4,128)} copy(f32[3,32768]{1,0:T(4,128)S(1)} %copy-done) | data formatting | bytes 786432
Async XLA Ops:
  54.6 3.3 %copy-start = (f32[3,32768]{1,0:T(4,128)S(1)}, f32[3,32768]{1,0:T(4,128)}, u32[]{:S(2)}) copy-start(f32[3,32768]{1,0:T(4,128)} %get-tuple-element.10) | copy-start | bytes 1179652

commit v4 on v2

--- a/solution.py
+++ b/solution.py
@@ -118,13 +118,13 @@
             ids = mlist[d:d + 1, pl.ds(at, chunk)]
             hot = one_hot(spread16((ids // LANES).astype(F32)), groups, iota_c)
             here = lane_no == (ids % LANES).astype(F32)
+            whole = jnp.dot(gt_hi[...], hot, preferred_element_type=F32)
+            low = jnp.dot(gt_lo[...], hot, preferred_element_type=F32)
             got = []
             for f in range(8):
-                part = jnp.dot(gt_hi[f * LANES:(f + 1) * LANES, :], hot, preferred_element_type=F32)
+                part = whole[f * LANES:(f + 1) * LANES]
                 if f < 7:
-                    part = part + jnp.dot(
-                        gt_lo[f * LANES:(f + 1) * LANES, :], hot, preferred_element_type=F32
-                    )
+                    part = part + low[f * LANES:(f + 1) * LANES]
                 got.append(jnp.sum(jnp.where(here, part, 0.0), axis=0, keepdims=True))
             gath[:, pl.ds(at, chunk)] = jnp.concatenate(got, axis=0)
             return carry
@@ -146,26 +146,26 @@
         slot_hot = one_hot(spread16(mslot[d:d + 1, :].astype(F32)), slots, iota16)
         block_rows = lax.dot_general(slot_hot, b0[:, :migs], NT, preferred_element_type=F32)
         rows[d, 0:slots, :] = block_rows[:, :4 * LANES] + block_rows[:, 4 * LANES:]
-        rows[d, slots:slots + 1, 0:slots] = side[d:d + 1, :].astype(F32)
-
-    iota_l = iota16[:, :LANES]
+        ids = side[d:d + 1, :].astype(F32)
+        rows[d, slots:slots + 8, :] = jnp.zeros((8, 4 * LANES), F32)
+        rows[d, slots:slots + 1, d * slots:(d + 1) * slots] = ids
+        rows[d, slots:slots + 1, (4 + d) * slots:(5 + d) * slots] = ids
+
+    cell_no = iota16[:, :LANES]
+    height_no = jnp.stack([cell_no + float(16 * k) for k in range(LANES // 16)], axis=0)
+    group_row_no = jnp.stack([cell_no + float(16 * k) for k in range(row_count // 16)], axis=0)
+    nought, one = jnp.zeros((), BF16), jnp.ones((), BF16)
 
     def build(group0, b, a):
         for k in range(GROUP):
             g = group0 + k
             cols = slice(k * LANES, (k + 1) * LANES)
-            h16 = spread16(tabs[8, pl.ds(g, 1), :])
-            r16 = spread16(tabs[9, pl.ds(g, 1), :])
-            hits = [iota_l == h16 - float(16 * block) for block in range(LANES // 16)]
+            hits = height_no == spread16(tabs[8, pl.ds(g, 1), :])[None]
             for p in range(8):
                 v16 = spread16(tabs[p, pl.ds(g, 1), :])
-                for block in range(LANES // 16):
-                    base = p * LANES + block * 16
-                    b[base:base + 16, cols] = jnp.where(hits[block], v16, jnp.zeros((), BF16))
-            for block in range(row_count // 16):
-                a[block * 16:(block + 1) * 16, cols] = jnp.where(
-                    iota_l == r16 - float(16 * block), jnp.ones((), BF16), jnp.zeros((), BF16)
-                )
+                b[p * LANES:(p + 1) * LANES, cols] = jnp.where(hits, v16[None], nought).reshape(LANES, LANES)
+            hits = group_row_no == spread16(tabs[9, pl.ds(g, 1), :])[None]
+            a[:, cols] = jnp.where(hits, one, nought).reshape(row_count, LANES)
 
     def add(b, a):
         acc[...] += lax.dot_general(b[...], a[...], NT, preferred_element_type=F32)
@@ -336,15 +336,14 @@
         send(mov.at[d], got_mov.at[d], mov_send.at[d], mov_recv.at[d], near[d]) for d in range(4)
     ]
 
-    extra = jnp.zeros((wide_x * wide_y, 4 * LANES), F32)
-    row_no = lax.broadcasted_iota(jnp.int32, (wide_x * wide_y, slots), 0).astype(F32)
     for d in range(4):
         row_copies[d].wait_recv()
-        ids = got_rows[d, slots:slots + 1, 0:slots]
-        hot = jnp.where(row_no == ids, 1.0, 0.0).astype(BF16)
-        hi, lo = parts_of(got_rows[d, 0:slots, :])
-        extra = extra + jnp.dot(hot, hi, preferred_element_type=F32)
-        extra = extra + jnp.dot(hot, lo, preferred_element_type=F32)
+    row_no = lax.broadcasted_iota(jnp.int32, (wide_x * wide_y, 8 * slots), 0).astype(F32)
+    ids = sum(got_rows[d, slots:slots + 1, 0:8 * slots] for d in range(4))
+    hot = jnp.where(row_no == ids, 1.0, 0.0).astype(BF16)
+    pieces = [parts_of(got_rows[d, 0:slots, :]) for d in range(4)]
+    depth = jnp.concatenate([p[0] for p in pieces] + [p[1] for p in pieces], axis=0)
+    extra = jnp.dot(hot, depth, preferred_element_type=F32)
     fraction = 1.0 / (1.0 + (dep[3] + extra[:, 3 * LANES:]))
     phi[...] = fraction.reshape(1, wide_x, wide_y, LANES)
     second = send_faces(1, phi, 1)

time: 65 us -> 64.4 us (level)
  no operation moved by 1% of the time
where the time goes in v4:
time: 64.4 us; the launch traced here: 64.1 us
  Pallas kernels  59.3 us (92%)
  local copies, waits for them, and re-layouts  4.21 us (7%)
  between operations  0.66 us (1%)
    pallas_call x1, Pallas kernels, local_part(): pl.pallas_call(local_kernel, out_shape=(jax.ShapeDtypeStruct((3, fibres),...  36.7 us
    pallas_call x1, Pallas kernels, sweeps(): pl.pallas_call(sweep_kernel, out_shape=(jax.ShapeDtypeStruct(velocity.sha...  22.6 us
    unnamed x10, local copies, waits for them, and re-layouts  4.21 us

profile of v4, /device:TPU:0, one launch (start us, length us, event | category | flops | bytes accessed | tf_op | source)
XLA Modules:
  0.0 64.1 jit_solution(16574923551573835739)
XLA Ops:
  0.6 0.0 copy-start.1
  0.6 36.7 %fibres.1 = (f32[3,32768]{1,0:T(4,128)}, f32[4,256,128]{2,1,0:T(8,128)}, f32[4,24,512]{2,1,0:T(8,128)}, f32[4,3,1024]{2,1,0:T(4,128)}) custom-call(f32[3,32768]{1,0:T(4,128)} %vel.1, f32[3,32768]{1,0:T(4,128)} %flu.1, f32[2,32768]{1,0:T(2,128)} %prop.1, s32[256,128]{1,0:T(8,128)} %bitcast.2, s32[256,128]{1,0:T(8,128)} %bitcast.3, s32[4,1024]{1,0:T(4,128)} %mlist.1, ...), custom_call_target="tpu_custom_call" | custom-call | flops 16999999488 | bytes 3000000 | tf_op jit(solution)/shard_map/fibres/pallas_call | solution.py:197
  37.4 0.0 copy-done.1
  37.4 0.0 copy-start
  37.4 1.0 %copy-done = f32[4,256,128]{2,1,0:T(8,128)S(1)} copy-done((f32[4,256,128]{2,1,0:T(8,128)S(1)}, f32[4,256,128]{2,1,0:T(8,128)}, u32[]{:S(2)}) %copy-start) | copy-done | bytes 524312
  38.4 0.0 copy-start.2
  38.4 0.9 %copy-done.2 = f32[4,24,512]{2,1,0:T(8,128)S(1)} copy-done((f32[4,24,512]{2,1,0:T(8,128)S(1)}, f32[4,24,512]{2,1,0:T(8,128)}, u32[]{:S(2)}) %copy-start.2) | copy-done | bytes 196632
  39.3 0.0 copy-start.3
  39.3 0.8 %copy-done.3 = f32[4,3,1024]{2,1,0:T(4,128)S(1)} copy-done((f32[4,3,1024]{2,1,0:T(4,128)S(1)}, f32[4,3,1024]{2,1,0:T(4,128)}, u32[]{:S(2)}) %copy-start.3) | copy-done | bytes 49176
  40.2 22.6 %sweeps.1 = (f32[3,8,32,128]{3,2,1,0:T(8,128)S(1)}, f32[4,3,1024]{2,1,0:T(4,128)S(1)}) custom-call(f32[3,8,32,128]{3,2,1,0:T(8,128)S(1)} %copy-done.1, f32[4,256,128]{2,1,0:T(8,128)S(1)} %copy-done, f32[4,24,512]{2,1,0:T(8,128)S(1)} %copy-done.2, f32[4,3,1024]{2,1,0:T(4,128)S(1)} %copy-done.3), custom_call_target="tpu_custom_call" | custom-call | flops 20000000 | bytes 2000000 | tf_op jit(solution)/shard_map/sweeps/pallas_call | solution.py:395
  62.7 0.7 %copy.12 = f32[4,3,1024]{2,0,1:T(4,128)} copy(f32[4,3,1024]{2,1,0:T(4,128)S(1)} %get-tuple-element.17) | data formatting | bytes 98304
  63.4 0.7 %copy.14 = f32[3,8,32,128]{3,2,1,0:T(8,128)} copy(f32[3,8,32,128]{3,2,1,0:T(8,128)S(1)} %get-tuple-element.21) | data formatting | bytes 786432
Async XLA Ops:
  0.6 36.7 %copy-start.1 = (f32[3,8,32,128]{3,2,1,0:T(8,128)S(1)}, f32[3,8,32,128]{3,2,1,0:T(8,128)}, u32[]{:S(2)}) copy-start(f32[3,8,32,128]{3,2,1,0:T(8,128)} %velocity.1) | copy-start | bytes 1179652
  37.4 1.0 %copy-start = (f32[4,256,128]{2,1,0:T(8,128)S(1)}, f32[4,256,128]{2,1,0:T(8,128)}, u32[]{:S(2)}) copy-start(f32[4,256,128]{2,1,0:T(8,128)} %get-tuple-element.9.dep) | copy-start | bytes 1572868
  38.4 0.9 %copy-start.2 = (f32[4,24,512]{2,1,0:T(8,128)S(1)}, f32[4,24,512]{2,1,0:T(8,128)}, u32[]{:S(2)}) copy-start(f32[4,24,512]{2,1,0:T(8,128)} %get-tuple-element.10.rows) | copy-start | bytes 589828
  39.3 0.8 %copy-start.3 = (f32[4,3,1024]{2,1,0:T(4,128)S(1)}, f32[4,3,1024]{2,1,0:T(4,128)}, u32[]{:S(2)}) copy-start(f32[4,3,1024]{2,1,0:T(4,128)} %get-tuple-element.11.mov) | copy-start | bytes 147460
